TPU v7x, 32 devices: a whole 2x2x4 slice. The times are simulated.
32 devices in a mesh: dp: 4 (over y, x), ctx: 2 (over core), tensor: 4 (over z).
Axes of the slice: x: 2, y: 2, z: 4, core: 2. Of those that a mesh axis runs over, the one named last changes fastest.
Arguments:
- tokens: bfloat16 [8192, 1024], P(('dp', 'ctx'), 'tensor'), may hold values from -6 to 6
- span_of_slot: int32 [4], replicated, may hold values from 0 to 3, each once
- norm_gain: bfloat16 [2, 1024], replicated, may hold values from 0.25 to 1.75
- norm_bias: bfloat16 [2, 1024], replicated, may hold values from -1 to 1
- qkv_weight: bfloat16 [3, 1024, 1024], P(None, None, 'tensor'), may hold values from -0.25 to 0.25
- qkv_bias: bfloat16 [3, 1024], P(None, 'tensor'), may hold values from -1 to 1
- attn_out_weight: bfloat16 [1024, 1024], P('tensor'), may hold values from -0.75 to 0.75
- out_bias: bfloat16 [2, 1024], P(None, 'tensor'), may hold values from -1 to 1
- mlp_in_weight: bfloat16 [1024, 4096], P(None, 'tensor'), may hold values from -0.1875 to 0.1875
- mlp_in_bias: bfloat16 [4096], P('tensor'), may hold values from -1 to 1
- mlp_out_weight: bfloat16 [4096, 1024], P('tensor'), may hold values from -0.09375 to 0.09375
- cotangent: bfloat16 [8192, 1024], P(('dp', 'ctx'), 'tensor'), may hold values from -6 to 6
Outputs:
- mixed: bfloat16 [8192, 1024], P(('dp', 'ctx'), 'tensor')
- input_grad: float32 [8192, 1024], P(('dp', 'ctx'), 'tensor')
- norm_gain_grad: float32 [2, 1024], P(None, 'tensor')
- norm_bias_grad: float32 [2, 1024], P(None, 'tensor')
- qkv_weight_grad: float32 [3, 1024, 1024], P(None, None, 'tensor')
- qkv_bias_grad: float32 [3, 1024], P(None, 'tensor')
- attn_out_weight_grad: float32 [1024, 1024], P('tensor')
- out_bias_grad: float32 [2, 1024], P(None, 'tensor')
- mlp_in_weight_grad: float32 [1024, 4096], P(None, 'tensor')
- mlp_in_bias_grad: float32 [4096], P('tensor')
- mlp_out_weight_grad: float32 [4096, 1024], P('tensor')
Inputs may be any that keep to these rules, and one draw needn't show every extreme that they name: A permutation: slot s, the block s % 2 of the two blocks of 512 rows of every sequence on index s // 2 of ctx, holds the positions span_of_slot[s] * 512 to span_of_slot[s] * 512 + 511 of that sequence.
All inputs are finite; a program needn't handle non-finite values.
Results may differ from a plain program's by a relative error of at most 0.008.
The roundings to bfloat16 on the way count: a program that leaves them out, or rounds other values in their place, can miss the bound.
Values may be sent and summed in bfloat16 or wider, within the bound.
A program may use at most 192 MiB of HBM per device.

v0:
```python
import jax
import jax.numpy as jnp
from jax import lax
from jax.sharding import PartitionSpec as P

HEAD = 64
ROT = 16
LEN = 2048


def norm_forward(full_rows):
    average = jnp.mean(full_rows, axis=-1, keepdims=True)
    centred = full_rows - average
    variance = jnp.mean(centred * centred, axis=-1, keepdims=True)
    inverse_scale = lax.rsqrt(variance + 1e-05)
    return (centred * inverse_scale, inverse_scale)


def norm_back(grad_rows, normed, inverse_scale, gain_row):
    scaled_grad = grad_rows * gain_row
    centre_term = jnp.mean(scaled_grad, axis=-1, keepdims=True)
    slope_term = jnp.mean(scaled_grad * normed, axis=-1, keepdims=True)
    return inverse_scale * (scaled_grad - centre_term - normed * slope_term)


def rotation_tables(positions):
    half_rot = ROT // 2
    frequency = 10000.0 ** (-2.0 * jnp.arange(half_rot, dtype=jnp.float32) / ROT)
    angle_rows = positions.astype(jnp.float32)[:, None] * frequency[None, :]
    return (jnp.cos(angle_rows)[:, None, :], jnp.sin(angle_rows)[:, None, :])


def rotate(field, cosine, sine):
    half_rot = cosine.shape[-1]
    lower_part = field[..., :half_rot]
    upper_part = field[..., half_rot : 2 * half_rot]
    return jnp.concatenate(
        [
            lower_part * cosine - upper_part * sine,
            upper_part * cosine + lower_part * sine,
            field[..., 2 * half_rot :],
        ],
        axis=-1,
    )


def rotate_back(field, cosine, sine):
    half_rot = cosine.shape[-1]
    lower_part = field[..., :half_rot]
    upper_part = field[..., half_rot : 2 * half_rot]
    return jnp.concatenate(
        [
            lower_part * cosine + upper_part * sine,
            upper_part * cosine - lower_part * sine,
            field[..., 2 * half_rot :],
        ],
        axis=-1,
    )


def local(
    tokens,
    span_of_slot,
    norm_gain,
    norm_bias,
    qkv_weight,
    qkv_bias,
    attn_out_weight,
    out_bias,
    mlp_in_weight,
    mlp_in_bias,
    mlp_out_weight,
    cotangent,
):
    full_tokens, full_grads = (
        lax.all_gather(tokens, "tensor", axis=1, tiled=True),
        lax.all_gather(cotangent, "tensor", axis=1, tiled=True),
    )
    tok_rows, local_width = tokens.shape
    ctx_count = lax.axis_size("ctx")
    span_len = LEN // (2 * ctx_count)
    seq_count = tok_rows // (2 * span_len)
    head_width = qkv_weight.shape[2]
    head_count = head_width // HEAD
    slot_table = span_of_slot.reshape(ctx_count, 2)
    offsets = jnp.arange(span_len, dtype=jnp.int32)
    own_spans = lax.dynamic_slice_in_dim(slot_table, lax.axis_index("ctx"), 1, 0)[0]
    query_pos = (own_spans[:, None] * span_len + offsets[None, :]).reshape(2 * span_len)
    cosine, sine = rotation_tables(query_pos)
    four_shape = (seq_count, 2 * span_len, head_count, HEAD)
    inputs = full_tokens.astype(jnp.float32)
    normed, inverse_scale = norm_forward(inputs)
    gains = norm_gain.astype(jnp.float32)
    shifts = norm_bias.astype(jnp.float32)
    norm_first = (normed * gains[0] + shifts[0]).astype(jnp.bfloat16)
    norm_second = (normed * gains[1] + shifts[1]).astype(jnp.bfloat16)
    projected = (
        jnp.einsum("td,cde->cte", norm_first, qkv_weight, preferred_element_type=jnp.float32)
        + qkv_bias.astype(jnp.float32)[:, None, :]
    )
    query_b = rotate(projected[0].reshape(four_shape), cosine, sine).astype(jnp.bfloat16)
    key_b = (
        rotate(projected[1].reshape(four_shape), cosine, sine)
        .astype(jnp.bfloat16)
        .reshape(tok_rows, head_width)
    )
    value_b = projected[2].astype(jnp.bfloat16)

    def weights_for(key_piece):
        shard_count = key_piece.shape[0] // tok_rows
        key_five = key_piece.reshape(shard_count, seq_count, 2 * span_len, head_count, HEAD)
        key_pos = (slot_table[:, :, None] * span_len + offsets[None, None, :]).reshape(
            shard_count, 2 * span_len
        )
        raw = 0.125 * jnp.einsum(
            "sqhd,wskhd->shqwk", query_b, key_five, preferred_element_type=jnp.float32
        )
        allowed = key_pos[None, None, None, :, :] <= query_pos[None, None, :, None, None]
        return (jnp.where(allowed, jnp.exp(raw), 0.0), key_five)

    weight, key_five = weights_for(lax.all_gather(key_b, "ctx", axis=0, tiled=True))
    value_five = lax.all_gather(value_b, "ctx", axis=0, tiled=True).reshape(key_five.shape)
    total = jnp.einsum(
        "shqwk,wskhd->sqhd",
        weight.astype(jnp.bfloat16),
        value_five,
        preferred_element_type=jnp.float32,
    )
    mass = jnp.sum(weight, axis=(3, 4))
    total, mass = (total, mass)
    mass_rows = mass.transpose(0, 2, 1)[..., None]
    attended = total / mass_rows
    attended_b = attended.reshape(tok_rows, head_width).astype(jnp.bfloat16)
    hidden = jnp.dot(
        norm_second, mlp_in_weight, preferred_element_type=jnp.float32
    ) + mlp_in_bias.astype(jnp.float32)
    activated_b = jax.nn.gelu(hidden, approximate=False).astype(jnp.bfloat16)
    branch_terms = jnp.dot(
        attended_b, attn_out_weight, preferred_element_type=jnp.float32
    ) + jnp.dot(activated_b, mlp_out_weight, preferred_element_type=jnp.float32)
    branch_sum = lax.psum_scatter(branch_terms, "tensor", scatter_dimension=1, tiled=True)
    bias_rows = out_bias.astype(jnp.float32)
    mixed = (tokens.astype(jnp.float32) + branch_sum + bias_rows[0] + bias_rows[1]).astype(
        jnp.bfloat16
    )
    grad_local = cotangent.astype(jnp.float32)
    column_sums = jnp.sum(grad_local, axis=0)
    out_bias_term = jnp.stack([column_sums, column_sums])
    attn_out_term = jnp.dot(attended_b.T, full_grads, preferred_element_type=jnp.float32)
    mlp_out_term = jnp.dot(activated_b.T, full_grads, preferred_element_type=jnp.float32)
    grad_attended = jnp.dot(
        full_grads, attn_out_weight.T, preferred_element_type=jnp.float32
    ).reshape(four_shape)
    grad_activated = jnp.dot(full_grads, mlp_out_weight.T, preferred_element_type=jnp.float32)
    normal_cdf = 0.5 * (1.0 + lax.erf(hidden * 0.7071067811865476))
    density = jnp.exp(-0.5 * hidden * hidden) * 0.3989422804014327
    grad_hidden = (grad_activated * (normal_cdf + hidden * density)).astype(jnp.bfloat16)
    mlp_in_bias_term = jnp.sum(grad_hidden.astype(jnp.float32), axis=0)
    mlp_in_term = jnp.dot(norm_second.T, grad_hidden, preferred_element_type=jnp.float32)
    second_part = jnp.dot(grad_hidden, mlp_in_weight.T, preferred_element_type=jnp.float32)
    scaled_b = (grad_attended / mass_rows).astype(jnp.bfloat16)
    corr_rows = jnp.sum(grad_attended * attended, axis=-1) / mass_rows[..., 0]
    correction = corr_rows.transpose(0, 2, 1)[..., None, None]
    key_all, value_all = (
        lax.all_gather(key_b, "ctx", axis=0, tiled=True),
        lax.all_gather(value_b, "ctx", axis=0, tiled=True),
    )
    weight, key_five = weights_for(key_all)
    value_five = value_all.reshape(key_five.shape)
    grad_weight = jnp.einsum(
        "sqhd,wskhd->shqwk", scaled_b, value_five, preferred_element_type=jnp.float32
    )
    grad_raw = (weight * (grad_weight - correction)).astype(jnp.bfloat16)
    grad_query = 0.125 * jnp.einsum(
        "shqwk,wskhd->sqhd", grad_raw, key_five, preferred_element_type=jnp.float32
    )
    grad_key = 0.125 * jnp.einsum(
        "shqwk,sqhd->wskhd", grad_raw, query_b, preferred_element_type=jnp.float32
    )
    grad_value = jnp.einsum(
        "shqwk,sqhd->wskhd",
        weight.astype(jnp.bfloat16),
        scaled_b,
        preferred_element_type=jnp.float32,
    )
    key_total = ctx_count * tok_rows
    kv_terms = jnp.concatenate(
        [grad_key.reshape(key_total, head_width), grad_value.reshape(key_total, head_width)], axis=1
    )
    kv_back = lax.psum_scatter(kv_terms, "ctx", scatter_dimension=0, tiled=True)
    grad_proj = jnp.stack(
        [
            rotate_back(grad_query, cosine, sine).reshape(tok_rows, head_width),
            rotate_back(kv_back[:, :head_width].reshape(four_shape), cosine, sine).reshape(
                tok_rows, head_width
            ),
            kv_back[:, head_width:],
        ]
    ).astype(jnp.bfloat16)
    qkv_bias_term = jnp.sum(grad_proj.astype(jnp.float32), axis=1)
    qkv_term = jnp.einsum("td,cte->cde", norm_first, grad_proj, preferred_element_type=jnp.float32)
    first_part = jnp.einsum(
        "cte,cde->td", grad_proj, qkv_weight, preferred_element_type=jnp.float32
    )
    column_start = lax.axis_index("tensor") * local_width
    first_full, second_full = lax.psum((first_part, second_part), "tensor")
    back_rows = norm_back(first_full, normed, inverse_scale, gains[0]) + norm_back(
        second_full, normed, inverse_scale, gains[1]
    )
    input_grad = grad_local + lax.dynamic_slice_in_dim(back_rows, column_start, local_width, 1)
    norm_local = lax.dynamic_slice_in_dim(
        jnp.stack(
            [
                jnp.sum(first_full * normed, axis=0),
                jnp.sum(second_full * normed, axis=0),
                jnp.sum(first_full, axis=0),
                jnp.sum(second_full, axis=0),
            ]
        ),
        column_start,
        local_width,
        1,
    )
    summed_grads = lax.psum(
        (
            qkv_term,
            qkv_bias_term,
            attn_out_term,
            out_bias_term,
            mlp_in_term,
            mlp_in_bias_term,
            mlp_out_term,
            norm_local,
        ),
        ("dp", "ctx"),
    )
    norm_summed = summed_grads[7]
    return (
        mixed,
        input_grad,
        norm_summed[0:2],
        norm_summed[2:4],
        summed_grads[0],
        summed_grads[1],
        summed_grads[2],
        summed_grads[3],
        summed_grads[4],
        summed_grads[5],
        summed_grads[6],
    )


def solution(mesh):
    placed = (
        P(("dp", "ctx"), "tensor"),
        P(),
        P(),
        P(),
        P(None, None, "tensor"),
        P(None, "tensor"),
        P("tensor", None),
        P(None, "tensor"),
        P(None, "tensor"),
        P("tensor"),
        P("tensor", None),
        P(("dp", "ctx"), "tensor"),
    )
    return jax.shard_map(
        local,
        mesh=mesh,
        in_specs=placed,
        out_specs=(
            P(("dp", "ctx"), "tensor"),
            P(("dp", "ctx"), "tensor"),
            P(None, "tensor"),
            P(None, "tensor"),
            P(None, None, "tensor"),
            P(None, "tensor"),
            P("tensor", None),
            P(None, "tensor"),
            P(None, "tensor"),
            P("tensor"),
            P("tensor", None),
        ),
        check_vma=False,
    )
```

profile of v0, /device:TPU:0, one launch (start us, length us, event | category | flops | bytes accessed | tf_op | source)
XLA Modules:
  0.0 847.5 jit_solution(6499930185568993594)
XLA Ops:
  7.2 0.7 all-gather.6.cloned.1.call-update
  8.0 0.7 all-gather.10.cloned.1.call-update
  8.7 0.7 broadcast_in_dim_reshape.2
  9.6 0.7 convert_element_type.96
  10.3 0.8 fusion.71
  11.1 1.4 fusion.72
  12.6 45.9 %all-gather.6.cloned.1.call-done = bf16[1024,1024]{1,0:T(8,128)(2,1)} async-done(((bf16[1024,256]{1,0:T(8,128)(2,1)}), bf16[1024,1024]{1,0:T(8,128)(2,1)}) %all-gather.6.cloned.1.call-update) | async-done | bytes 2097168 | tf_op jit(solution)/shard_map/all_gather | solution.py:76
  58.6 2.1 convert_reduce_fusion
  60.7 2.3 fusion.4
  63.0 2.3 add_bitcast_fusion
  65.5 1.0 fusion.48
  67.0 0.8 pad_maximum_fusion.2
  68.0 2.3 broadcast_compare_fusion
  70.3 2.1 slice.167
  72.7 31.9 %all-gather.10.cloned.1.call-done = bf16[1024,1024]{1,0:T(8,128)(2,1)} async-done(((bf16[1024,256]{1,0:T(8,128)(2,1)}), bf16[1024,1024]{1,0:T(8,128)(2,1)}) %all-gather.10.cloned.1.call-update) | async-done | bytes 2097168 | tf_op jit(solution)/shard_map/all_gather | solution.py:77
  104.6 3.4 fusion.75
  108.0 6.0 all-gather.8.cloned.1.call-done
  114.1 1.8 reshape.296
  115.9 17.4 %fusion = (f32[4,1024]{1,0:T(4,128)}, f32[4,1024,2,1024]{1,3,2,0:T(8,128)}) fusion(pred[1024,2,1024]{0,2,1:T(8,128)(4,1)} %broadcast_compare_fusion, bf16[2,1024,4,64]{1,0,3,2:T(2,128)(2,1)S(1)} %reshape.296, bf16[1024,4,48]{0,2,1:T(8,128)(2,1)S(1)} %fusion.47, bf16[1024,4,8]{0,2,1:T(8,128)(2,1)} %get-tuple-element.74, bf16[1024,4,8]{0,2,1:T(8,128)(2,1)} %get-tuple-element.73), kind=kOutput, calls=%fused_computation.2 | convolution fusion | flops 1100476416 | bytes 37240832 | tf_op jit(solution)/shard_map/sqhd,wskhd->shqwk/dot_general | solution.py:115
  133.3 2.6 reshape.295
  135.9 16.2 %multiply_reduce_fusion.4 = (f32[1024,4]{0,1:T(4,128)}, bf16[1,1024,4,64]{1,3,2,0:T(8,128)(2,1)}) fusion(f32[1,1024,4,64]{1,3,2,0:T(8,128)} %bitcast.143, f32[1024,4]{0,1:T(4,128)} %bitcast.164, f32[4,1024,2,1024]{1,3,2,0:T(8,128)} %get-tuple-element.96, pred[1024,2,1024]{0,2,1:T(8,128)(4,1)} %broadcast_compare_fusion, bf16[2,1024,4,64]{1,0,3,2:T(2,128)(2,1)} %reshape.295), kind=kOutput, calls=%fused_computation.71 | convolution fusion | flops 1099952128 | bytes 38305792 | tf_op jit(solution)/shard_map/shqwk,wskhd->sqhd/dot_general | solution.py:123
  152.1 1.3 fusion.50
  153.5 15.8 %convolution_bitcast_fusion.2 = f32[2,1,1024,4,64]{2,4,0,3,1:T(8,128)} fusion(f32[4,1024,2,1024]{1,3,2,0:T(8,128)} %get-tuple-element.96, pred[1024,2,1024]{0,2,1:T(8,128)(4,1)} %broadcast_compare_fusion, f32[1024,4,64]{0,2,1:T(8,128)} %bitcast.144, f32[1024,4]{0,1:T(4,128)} %bitcast.165), kind=kOutput, calls=%fused_computation.53 | convolution fusion | flops 1099431936 | bytes 38813696 | tf_op jit(solution)/shard_map/shqwk,sqhd->wskhd/dot_general | solution.py:180
  169.3 20.5 %multiply_convert_fusion = bf16[4,1024,2,1024]{1,3,2,0:T(8,128)(2,1)} fusion(f32[4,1024,2,1024]{1,3,2,0:T(8,128)} %get-tuple-element.96, f32[4,1024]{1,0:T(4,128)} %fusion.50, pred[1024,2,1024]{0,2,1:T(8,128)(4,1)} %broadcast_compare_fusion, bf16[2,1024,4,64]{1,0,3,2:T(2,128)(2,1)} %reshape.295, f32[1024,4,64]{0,2,1:T(8,128)} %bitcast.145, f32[1024,4]{0,1:T(4,128)} %bitcast.166), kind=kOutput, calls=%fused_computation | convolution fusion | flops 1116209152 | bytes 54558720 | tf_op jit(solution)/shard_map/sqhd,wskhd->shqwk/dot_general | solution.py:170
  189.8 12.4 %multiply_bitcast_fusion = f32[2,1,1024,4,64]{2,4,0,3,1:T(8,128)} fusion(bf16[4,1024,2,1024]{1,3,2,0:T(8,128)(2,1)} %multiply_convert_fusion, bf16[1024,4,48]{0,2,1:T(8,128)(2,1)S(1)} %fusion.47, bf16[1024,4,8]{0,2,1:T(8,128)(2,1)} %get-tuple-element.74, bf16[1024,4,8]{0,2,1:T(8,128)(2,1)} %get-tuple-element.73), kind=kOutput, calls=%fused_computation.49 | convolution fusion | flops 1075838976 | bytes 19398656 | tf_op jit(solution)/shard_map/shqwk,sqhd->wskhd/dot_general | solution.py:177
  202.1 4.7 copy.66
  206.9 5.3 reshape.310
  212.2 4.7 copy.67
  216.9 5.3 reshape.311
  222.2 4.8 pad_maximum_fusion
  227.6 14.5 %fusion.7 = (bf16[1024,1024]{1,0:T(8,128)(2,1)S(1)}, f32[1024,1024]{1,0:T(8,128)}) fusion(f32[1024]{0:T(1024)S(1)} %convert_element_type.104, bf16[1024,1024]{1,0:T(8,128)(2,1)S(1)} %copy-done, bf16[1024,1024]{1,0:T(8,128)(2,1)} %all-gather.6.cloned.1.call-done, f32[1024]{0:T(1024)S(1)} %bitcast.173, f32[1024]{0:T(1024)S(1)} %bitcast.157, ...), kind=kOutput, calls=%fused_computation.13 | convolution fusion | flops 2222981120 | bytes 10506240 | tf_op jit(solution)/shard_map/dot_general | solution.py:134
  242.2 2.3 fusion.74
  244.6 2.8 convolution_add_fusion
  247.5 6.7 fusion.78
  254.2 4.7 convert_reduce_fusion.1
  259.0 1.3 copy-done.29
  260.3 4.8 fusion.62
  265.1 3.0 fusion.29
  268.1 1.0 copy-done.5
  269.2 1.7 fusion.77
  270.9 1.3 slice.126
  272.2 1.3 copy.50
  273.5 1.2 slice.168
  274.7 1.2 add_convert_fusion.4
  275.9 0.9 pad_maximum_fusion.3
  277.0 1.2 copy.52
  278.3 1.5 fusion.44
  279.8 0.8 copy-done.13
  280.6 5.4 convolution_bitcast_fusion.1
  286.3 6.1 fusion.76
  292.4 3.8 convolution_bitcast_fusion
  296.2 0.6 copy-done.21
  296.9 1.4 convert_reduce_fusion.2
  298.3 27.1 %reduce-scatter.3.cloned.1.call-done = f32[1024,256]{1,0:T(8,128)} async-done(((f32[1024,1024]{1,0:T(8,128)}), f32[1024,256]{1,0:T(8,128)}) %reduce-scatter.3.cloned.1.call-update) | async-done | bytes 1048592 | tf_op jit(solution)/shard_map/reduce_scatter | solution.py:141
  325.5 2.2 add_convert_fusion.2
  327.7 176.3 %all-reduce.6.cloned.1.call-done = (f32[3,1024,256]{1,2,0:T(8,128)}, f32[256,1024]{1,0:T(8,128)}, f32[1024,1024]{1,0:T(8,128)}, f32[1024,1024]{1,0:T(8,128)}) async-done(((f32[3,1024,256]{1,2,0:T(8,128)}, f32[256,1024]{1,0:T(8,128)}, f32[1024,1024]{1,0:T(8,128)}, f32[1024,1024]{1,0:T(8,128)}), (f32[3,1024,256]{1,2,0:T(8,128)}, f32[256,1024]{1,0:T(8,128)}, f32[1024,1024]{1,0:T(8,128)}, ...) | async-done | bytes 12582928 | tf_op jit(solution)/shard_map/psum | solution.py:224
  503.9 3.5 copy.54
  507.5 291.5 %all-reduce.8.cloned.1.call-done = (f32[1024,1024]{1,0:T(8,128)}, f32[1024,1024]{1,0:T(8,128)}) async-done(((f32[1024,1024]{1,0:T(8,128)}, f32[1024,1024]{1,0:T(8,128)}), (f32[1024,1024]{1,0:T(8,128)}, f32[1024,1024]{1,0:T(8,128)})) %all-reduce.8.cloned.1.call-update) | async-done | bytes 8388624 | tf_op jit(solution)/shard_map/psum | solution.py:206
  799.0 6.4 fusion.64
  805.5 1.7 convert_reduce_fusion.3
  807.3 24.6 %all-reduce = (f32[4,256]{1,0:T(4,128)S(1)}, f32[3,256]{1,0:T(4,128)}, f32[2,256]{1,0:T(2,128)}, f32[1024]{0:T(1024)}) all-reduce(f32[4,256]{1,0:T(4,128)S(1)} %fusion.53, f32[3,256]{1,0:T(4,128)S(1)} %convert_reduce_fusion.2, f32[2,256]{1,0:T(2,128)S(1)} %pad_maximum_fusion.5, ...), channel_id=1, replica_groups=mesh['dp'=4,'ctx'=2,'tensor'=4] {'dp','ctx'}, use_global_device_ids=true, to_apply=%region_16.17 | all-reduce | flops 3328 | bytes 26624 | tf_op jit(solution)/shard_map/psum | solution.py:224
  832.5 1.0 copy.91
  833.4 4.9 copy.92
  838.4 2.0 copy.93
  (113 shorter events, 3.7 us)
Async XLA Ops:
  7.2 220.5 %copy-start = (bf16[1024,1024]{1,0:T(8,128)(2,1)S(1)}, bf16[1024,1024]{1,0:T(8,128)(2,1)}, u32[]{:S(2)}) copy-start(bf16[1024,1024]{1,0:T(8,128)(2,1)} %param.20) | copy-start | bytes 6291460
  7.2 51.4 %all-gather.6.cloned.1.call-start = ((), (), s32[]{:S(2)}) async-start(), calls=%async_computation.2 | async-start | bytes 2621440 | tf_op jit(solution)/shard_map/all_gather | solution.py:76
  7.9 96.7 %all-gather.10.cloned.1.call-start = ((), (), s32[]{:S(2)}) async-start(), calls=%async_computation.5 | async-start | bytes 2621440 | tf_op jit(solution)/shard_map/all_gather | solution.py:77
  8.7 105.4 %all-gather.8.cloned.1.call-start = ((), (), s32[]{:S(2)}) async-start(), calls=%async_computation.3 | async-start | bytes 1572864 | tf_op jit(solution)/shard_map/all_gather | solution.py:121
  11.0 54.2 %copy-start.18 = (f32[1,1024]{1,0:T(1,128)}, f32[1,1024]{1,0:T(1,128)S(1)}, u32[]{:S(2)}) copy-start(f32[1,1024]{1,0:T(1,128)S(1)} %get-tuple-element.89) | copy-start | bytes 12292
  12.4 52.8 %copy-start.22 = (f32[1,1024]{1,0:T(1,128)}, f32[1,1024]{1,0:T(1,128)S(1)}, u32[]{:S(2)}) copy-start(f32[1,1024]{1,0:T(1,128)S(1)} %get-tuple-element.91) | copy-start | bytes 12292
  12.6 52.8 %copy-start.16 = (f32[1024,8]{0,1:T(8,128)}, f32[1024,8]{0,1:T(8,128)S(1)}, u32[]{:S(2)}) copy-start(f32[1024,8]{0,1:T(8,128)S(1)} %get-tuple-element.85) | copy-start | bytes 98308
  12.6 52.8 %copy-start.17 = (f32[1024,8]{0,1:T(8,128)}, f32[1024,8]{0,1:T(8,128)S(1)}, u32[]{:S(2)}) copy-start(f32[1024,8]{0,1:T(8,128)S(1)} %get-tuple-element.86) | copy-start | bytes 98308
  58.6 4.4 copy-start.1
  58.6 4.4 copy-start.27
  65.3 1.7 copy-start.6
  67.8 65.5 %all-gather.12.cloned.1.call-start = ((), (), s32[]{:S(2)}) async-start(), calls=%async_computation.7 | async-start | bytes 1572864 | tf_op jit(solution)/shard_map/all_gather | solution.py:122
  72.4 198.4 %reduce-scatter.5.cloned.1.call-start = ((), (), s32[]{:S(2)}) async-start(), calls=%async_computation.6 | async-start | bytes 6291456 | tf_op jit(solution)/shard_map/reduce_scatter | solution.py:190
  226.9 0.7 copy-start.24
  226.9 0.7 copy-start.23
  227.0 98.5 %reduce-scatter.3.cloned.1.call-start = ((), (), s32[]{:S(2)}) async-start(), calls=%async_computation.4 | async-start | bytes 5242880 | tf_op jit(solution)/shard_map/reduce_scatter | solution.py:141
  227.6 14.6 %copy-start.25 = (bf16[1024,1024]{1,0:T(8,128)(2,1)S(1)}, bf16[1024,1024]{1,0:T(8,128)(2,1)}, u32[]{:S(2)}) copy-start(bf16[1024,1024]{1,0:T(8,128)(2,1)} %param.22) | copy-start | bytes 6291460
  242.2 2.4 copy-start.30
  242.2 2.4 copy-start.7
  242.2 2.4 copy-start.8
  247.4 256.6 %all-reduce.6.cloned.1.call-start = ((), (), s32[]{:S(2)}) async-start(), calls=%async_computation.8 | async-start | bytes 25165824 | tf_op jit(solution)/shard_map/psum | solution.py:224
  247.4 6.7 copy-start.3
  247.4 6.7 copy-start.26
  247.5 6.7 copy-start.31
  254.2 6.1 copy-start.2
  254.2 10.9 %slice-start = ((s8[16777216]{0:T(1024)(128)(4,1)}), s8[4194304]{0:T(1024)(128)(4,1)S(1)}, s32[]{:S(2)}) async-start(s8[16777216]{0:T(1024)(128)(4,1)} %bitcast.135), calls=%async_computation.10 | async-start | bytes 8388608
  254.2 10.9 %slice-start.1 = ((s8[16777216]{0:T(1024)(128)(4,1)}), s8[4194304]{0:T(1024)(128)(4,1)S(1)}, s32[]{:S(2)}) async-start(s8[16777216]{0:T(1024)(128)(4,1)} %bitcast.135), calls=%async_computation.11 | async-start | bytes 8388608
  254.2 10.8 %slice-start.2 = ((s8[16777216]{0:T(1024)(128)(4,1)}), s8[4194304]{0:T(1024)(128)(4,1)S(1)}, s32[]{:S(2)}) async-start(s8[16777216]{0:T(1024)(128)(4,1)} %bitcast.135), calls=%async_computation.12 | async-start | bytes 8388608
  259.0 1.3 copy-start.29
  260.3 4.8 slice-start.3
  265.1 4.1 copy-start.9
  268.1 1.0 copy-start.5
  272.2 8.4 copy-start.19
  278.3 14.1 %copy-start.12 = (bf16[1,1024,256]{2,1,0:T(8,128)(2,1)}, bf16[1,1024,256]{2,1,0:T(8,128)(2,1)S(1)}, u32[]{:S(2)}) copy-start(bf16[1,1024,256]{2,1,0:T(8,128)(2,1)S(1)} %copy.52) | copy-start | bytes 1572868
  279.8 0.8 copy-start.13
  286.0 513.0 %all-reduce.8.cloned.1.call-start = ((), (), s32[]{:S(2)}) async-start(), calls=%async_computation.9 | async-start | bytes 16777216 | tf_op jit(solution)/shard_map/psum | solution.py:206
  286.2 6.1 copy-start.14
  286.2 6.1 copy-start.28
  296.2 0.7 copy-start.21
  296.2 29.3 %copy-start.10 = (bf16[1024,256]{1,0:T(8,128)(2,1)S(1)}, bf16[1024,256]{1,0:T(8,128)(2,1)}, u32[]{:S(2)}) copy-start(bf16[1024,256]{1,0:T(8,128)(2,1)} %param.12) | copy-start | bytes 1572868
  798.9 6.5 copy-start.11
  805.4 1.9 copy-start.20
  805.4 27.1 %copy-start.15 = (f32[256,1024]{1,0:T(8,128)S(1)}, f32[256,1024]{1,0:T(8,128)}, u32[]{:S(2)}) copy-start(f32[256,1024]{1,0:T(8,128)} %get-tuple-element.110) | copy-start | bytes 3145732
  833.4 4.9 copy-start.4
Sparse Core Ops, SparseCore 0:
  9.6 48.9 all-gather.5
  60.1 44.4 all-gather.9
  106.7 7.2 all-gather.7
  116.0 10.1 all-gather.11
  227.1 13.2 reduce-scatter.4
  247.5 77.9 reduce-scatter.2
  330.0 173.8 all-reduce.5
  507.3 291.6 all-reduce.7
where the time goes:
time: 853 us; the launch traced here: 847 us
  waiting for transfers between devices  580 us (68%)
  matrix products  144 us (17%)
  local copies, waits for them, and re-layouts  53.6 us (6%)
  other arithmetic  29.6 us (3%)
  blocking collectives  24.6 us (3%)
  between operations  14.9 us (2%)
    psum x1, waiting for transfers between devices, local(): first_full, second_full = lax.psum((first_part, second_part), 'tensor')  291 us
    psum x1, waiting for transfers between devices, local(): lax.psum((qkv_term, qkv_bias_term, attn_out_term, out_bias_term, mlp_in_t...  176 us
    all_gather x1, waiting for transfers between devices, local(): lax.all_gather(tokens, 'tensor', axis=1, tiled=True)  45.9 us
    all_gather x1, waiting for transfers between devices, local(): lax.all_gather(cotangent, 'tensor', axis=1, tiled=True)  31.9 us
    reduce_scatter x1, waiting for transfers between devices, local(): lax.psum_scatter(branch_terms, 'tensor', scatter_dimension=1, tiled=True)  27.1 us
    psum x1, blocking collectives, local(): lax.psum((qkv_term, qkv_bias_term, attn_out_term, out_bias_term, mlp_in_t...  24.6 us
    dot_general x1, matrix products, local(): jnp.einsum('sqhd,wskhd->shqwk', scaled_b, value_five, preferred_element_t...  20.5 us
    dot_general x1, matrix products, weights_for(): jnp.einsum('sqhd,wskhd->shqwk', query_b, key_five, preferred_element_type...  17.4 us
  transfers between devices with their start and end apart: 8, of which 6 were waited for; matrix products, arithmetic and copies ran while one was open for 13% of the time, Pallas kernels for 0%

commit v1 on v0

v1 whole, which is shorter than its diff:
```python
import functools

import jax
import jax.numpy as jnp
from jax import lax
from jax.experimental import pallas as pl
from jax.experimental.pallas import tpu as pltpu
from jax.sharding import PartitionSpec as P

HEAD = 64
ROT = 16
LEN = 2048
BF16 = jnp.bfloat16
F32 = jnp.float32


def line_gather(block, axis, pieces):
    size = lax.axis_size(axis)
    me = lax.axis_index(axis)
    width = block.shape[1]
    rows = block.shape[0] // pieces
    gathered = []
    for piece in range(pieces):
        own = block[piece * rows : (piece + 1) * rows]
        rising, falling, below, above = own, own, [], []
        for step in range(size - 1):
            rising = lax.ppermute(rising, axis, [(i, i + 1) for i in range(step, size - 1)])
            falling = lax.ppermute(falling, axis, [(i + 1, i) for i in range(size - 1 - step)])
            below.append(rising)
            above.append(falling)
        side = jnp.concatenate(below[::-1] + [own] + above, axis=1)
        gathered.append(
            lax.dynamic_slice_in_dim(side, (size - 1 - me) * width, size * width, 1)
        )
    return gathered


def line_scatter(terms, axis):
    size = lax.axis_size(axis)
    me = lax.axis_index(axis)
    width = terms.shape[1] // size

    def columns(owner):
        return lax.dynamic_slice_in_dim(terms, jnp.clip(owner, 0, size - 1) * width, width, 1)

    rising = falling = None
    for step in range(1, size):
        reach = size - step
        up, down = columns(me + reach), columns(me - reach)
        if rising is not None:
            up, down = up + rising.astype(F32), down + falling.astype(F32)
        rising = lax.ppermute(
            up.astype(BF16), axis, [(i, i + 1) for i in range(size - 1) if i + reach < size]
        )
        falling = lax.ppermute(
            down.astype(BF16), axis, [(i, i - 1) for i in range(1, size) if i - reach >= 0]
        )
    total = columns(me)
    if rising is not None:
        total = total + rising.astype(F32) + falling.astype(F32)
    return total


def swap(block, axis, bit):
    return lax.ppermute(block, axis, [(i, i ^ bit) for i in range(lax.axis_size(axis))])


def small_sum(block, axes):
    for axis in axes:
        bit = 1
        while bit < lax.axis_size(axis):
            block = block + swap(block, axis, bit)
            bit *= 2
    return block


def weight_sum(term):
    spans, groups = lax.axis_size("ctx"), lax.axis_size("dp")
    if spans != 2:
        return lax.psum(term, ("dp", "ctx"))
    core, chip = lax.axis_index("ctx"), lax.axis_index("dp")
    rows, width = term.shape
    shares = term.reshape(spans, groups, rows // (spans * groups), width)
    given = lax.dynamic_index_in_dim(shares, 1 - core, 0, False).astype(BF16)
    kept = lax.dynamic_index_in_dim(shares, core, 0, False) + swap(given, "ctx", 1).astype(F32)
    own = lax.dynamic_index_in_dim(kept, chip, 0, False)
    low = kept.astype(BF16)
    for bit in range(1, groups):
        own = own + swap(
            lax.dynamic_index_in_dim(low, chip ^ bit, 0, False), "dp", bit
        ).astype(F32)
    own = own.astype(BF16)
    whole = jnp.zeros(low.shape, BF16)
    whole = lax.dynamic_update_index_in_dim(whole, own, chip, 0)
    for bit in range(1, groups):
        whole = lax.dynamic_update_index_in_dim(whole, swap(own, "dp", bit), chip ^ bit, 0)
    other = swap(whole, "ctx", 1)
    first, second = jnp.where(core == 0, whole, other), jnp.where(core == 0, other, whole)
    return jnp.stack([first, second]).astype(F32).reshape(rows, width)


def attention_body(
    heads, chunk, qmax, kmin, q, g, k, v, qpos, kpos, att, dq, dk, dv, e_keep, mass, out, k_head, v_head
):
    block = pl.program_id(1)
    width = q.shape[-1]
    chunks = k.shape[1] // chunk
    lane = lax.broadcasted_iota(jnp.int32, (1, width), 1)
    picks = [((lane >= h * HEAD) & (lane < (h + 1) * HEAD)).astype(F32) for h in range(heads)]

    @pl.when(block == 0)
    def _():
        dk[...] = jnp.zeros_like(dk)
        dv[...] = jnp.zeros_like(dv)
        for h in range(heads):
            k_head[h] = k[0] * picks[h].astype(BF16)
            v_head[h] = v[0] * picks[h].astype(BF16)

    nt = (((1,), (1,)), ((), ()))
    tn = (((0,), (0,)), ((), ()))
    dq[...] = jnp.zeros_like(dq)
    queries = q[0]
    grads = g[0]
    result = jnp.zeros(grads.shape, F32)
    for h in range(heads):
        mass[...] = jnp.zeros_like(mass)
        out[...] = jnp.zeros_like(out)
        for c in range(chunks):
            part = pl.ds(c * chunk, chunk)

            @pl.when(kmin[c] <= qmax[block])
            def _():
                raw = lax.dot_general(queries, k_head[h, part], nt, preferred_element_type=F32)
                e = jnp.where(kpos[:, part] <= qpos[...], jnp.exp(raw), 0.0)
                e_keep[:, part] = e
                mass[...] += jnp.sum(e, axis=1, keepdims=True)
                out[...] += jnp.dot(e.astype(BF16), v_head[h, part], preferred_element_type=F32)

        inverse = 1.0 / mass[...]
        attended = out[...] * inverse
        result = result + attended
        scaled = (grads * inverse).astype(BF16)
        corr = jnp.sum(grads * attended, axis=1, keepdims=True) * inverse
        pick = picks[h].astype(BF16)
        scaled_head = scaled * pick
        q_head = queries * pick
        for c in range(chunks):
            part = pl.ds(c * chunk, chunk)

            @pl.when(kmin[c] <= qmax[block])
            def _():
                e = e_keep[:, part]
                slope = lax.dot_general(scaled, v_head[h, part], nt, preferred_element_type=F32)
                d_raw = (e * (slope - corr)).astype(BF16)
                dq[0] += jnp.dot(d_raw, k_head[h, part], preferred_element_type=F32)
                dk[0, part] += lax.dot_general(d_raw, q_head, tn, preferred_element_type=F32)
                dv[0, part] += lax.dot_general(
                    e.astype(BF16), scaled_head, tn, preferred_element_type=F32
                )

    att[0] = result.astype(BF16)


def attention(q, g, k, v, qpos, kpos):
    seqs, q_rows, width = q.shape
    k_rows = k.shape[1]
    heads = width // HEAD
    block, chunk = min(512, q_rows), min(512, k_rows)
    qmax = jnp.max(qpos.reshape(-1, block), axis=1)
    kmin = jnp.min(kpos.reshape(-1, chunk), axis=1)
    by_block = pl.BlockSpec((1, block, width), lambda s, b: (s, b, 0))
    by_seq = pl.BlockSpec((1, k_rows, width), lambda s, b: (s, 0, 0))
    smem = pl.BlockSpec(memory_space=pltpu.SMEM)
    pairs = seqs * q_rows * k_rows * width
    return pl.pallas_call(
        functools.partial(attention_body, heads, chunk),
        grid=(seqs, q_rows // block),
        in_specs=[
            smem,
            smem,
            by_block,
            by_block,
            by_seq,
            by_seq,
            pl.BlockSpec((block, 1), lambda s, b: (b, 0)),
            pl.BlockSpec((1, k_rows), lambda s, b: (0, 0)),
        ],
        out_specs=[by_block, by_block, by_seq, by_seq],
        out_shape=[
            jax.ShapeDtypeStruct(q.shape, BF16),
            jax.ShapeDtypeStruct(q.shape, F32),
            jax.ShapeDtypeStruct(k.shape, F32),
            jax.ShapeDtypeStruct(k.shape, F32),
        ],
        scratch_shapes=[
            pltpu.VMEM((block, k_rows), F32),
            pltpu.VMEM((block, 1), F32),
            pltpu.VMEM((block, width), F32),
            pltpu.VMEM((heads, k_rows, width), BF16),
            pltpu.VMEM((heads, k_rows, width), BF16),
        ],
        cost_estimate=pl.CostEstimate(
            flops=48 * pairs, bytes_accessed=16 * seqs * k_rows * width, transcendentals=pairs // HEAD
        ),
        compiler_params=pltpu.CompilerParams(vmem_limit_bytes=44 * 2**20),
    )(qmax, kmin, q, g, k, v, qpos[:, None], kpos[None, :])


def norm_forward(full_rows):
    average = jnp.mean(full_rows, axis=-1, keepdims=True)
    centred = full_rows - average
    variance = jnp.mean(centred * centred, axis=-1, keepdims=True)
    inverse_scale = lax.rsqrt(variance + 1e-05)
    return (centred * inverse_scale, inverse_scale)


def rotation_tables(positions, width):
    half_rot = ROT // 2
    dim = jnp.arange(width, dtype=jnp.int32) % HEAD
    frequency = 10000.0 ** (-2.0 * (dim % half_rot).astype(F32) / ROT)
    angle = positions.astype(F32)[:, None] * frequency[None, :]
    cosine = jnp.where(dim < ROT, jnp.cos(angle), 1.0)
    sine = jnp.sin(angle)
    lower = jnp.where(dim < half_rot, sine, 0.0)
    upper = jnp.where((dim >= half_rot) & (dim < ROT), sine, 0.0)
    return lax.optimization_barrier((cosine, lower, upper))


def rotate(field, tables, sign):
    cosine, lower, upper = tables
    half_rot = ROT // 2
    return (
        field * cosine
        - sign * jnp.roll(field, -half_rot, axis=1) * lower
        + sign * jnp.roll(field, half_rot, axis=1) * upper
    )


def local(
    tokens,
    span_of_slot,
    norm_gain,
    norm_bias,
    qkv_weight,
    qkv_bias,
    attn_out_weight,
    out_bias,
    mlp_in_weight,
    mlp_in_bias,
    mlp_out_weight,
    cotangent,
):
    tok_rows, local_width = tokens.shape
    ctx_count = lax.axis_size("ctx")
    span_len = LEN // (2 * ctx_count)
    seq_count = tok_rows // (2 * span_len)
    seq_rows = 2 * span_len
    head_width = qkv_weight.shape[2]
    column_start = lax.axis_index("tensor") * local_width

    full_tokens = jnp.concatenate(line_gather(tokens, "tensor", 2), axis=0)
    full_tokens, late_cotangent = lax.optimization_barrier((full_tokens, cotangent))
    full_grads = jnp.concatenate(line_gather(late_cotangent, "tensor", 2), axis=0)

    slot_table = span_of_slot.reshape(ctx_count, 2)
    offsets = jnp.arange(span_len, dtype=jnp.int32)

    def positions_of(spans):
        return (spans[..., None] * span_len + offsets).reshape(-1)

    own_spans = lax.dynamic_index_in_dim(slot_table, lax.axis_index("ctx"), 0, False)
    query_pos = positions_of(own_spans)
    tables = rotation_tables(jnp.tile(query_pos, seq_count), head_width)

    normed, inverse_scale = norm_forward(full_tokens.astype(F32))
    gains = norm_gain.astype(F32)
    shifts = norm_bias.astype(F32)
    norm_first = (normed * gains[0] + shifts[0]).astype(BF16)
    norm_second = (normed * gains[1] + shifts[1]).astype(BF16)

    projected = [
        jnp.dot(norm_first, qkv_weight[c], preferred_element_type=F32) + qkv_bias[c].astype(F32)
        for c in range(3)
    ]
    query_b = (rotate(projected[0], tables, 1.0).astype(BF16) * BF16(0.125)).reshape(
        seq_count, seq_rows, head_width
    )
    key_value = jnp.stack([rotate(projected[1], tables, 1.0).astype(BF16), projected[2].astype(BF16)])
    if ctx_count == 2:
        other_spans = lax.dynamic_index_in_dim(slot_table, 1 - lax.axis_index("ctx"), 0, False)
        key_pos = positions_of(jnp.concatenate([own_spans, other_spans]))
        shards = [key_value, swap(key_value, "ctx", 1)]
    else:
        key_pos = positions_of(span_of_slot)
        shards = list(lax.all_gather(key_value, "ctx"))
    key_value = jnp.concatenate(
        [shard.reshape(2, seq_count, seq_rows, head_width) for shard in shards], axis=2
    )

    hidden = jnp.dot(norm_second, mlp_in_weight, preferred_element_type=F32) + mlp_in_bias.astype(F32)
    normal_cdf = 0.5 * (1.0 + lax.erf(hidden * 0.7071067811865476))
    density = jnp.exp(-0.5 * hidden * hidden) * 0.3989422804014327
    activated_b, gelu_slope = lax.optimization_barrier(
        ((hidden * normal_cdf).astype(BF16), normal_cdf + hidden * density)
    )

    grad_local = cotangent.astype(F32)
    mlp_out_term = jnp.dot(activated_b.T, full_grads, preferred_element_type=F32)
    mlp_out_grad = weight_sum(mlp_out_term)
    grad_activated = jnp.dot(full_grads, mlp_out_weight.T, preferred_element_type=F32)
    grad_hidden = lax.optimization_barrier((grad_activated * gelu_slope).astype(BF16))
    mlp_in_term = jnp.dot(norm_second.T, grad_hidden, preferred_element_type=F32)
    mlp_in_grad = weight_sum(mlp_in_term)

    grad_attended = jnp.dot(full_grads, attn_out_weight.T, preferred_element_type=F32)
    attended_b, grad_query, grad_key, grad_value = attention(
        query_b,
        grad_attended.reshape(seq_count, seq_rows, head_width),
        key_value[0],
        key_value[1],
        query_pos,
        key_pos,
    )
    attended_b = attended_b.reshape(tok_rows, head_width)

    if ctx_count == 2:

        def to_owner(grad):
            return (grad[:, :seq_rows] + swap(grad[:, seq_rows:], "ctx", 1)).reshape(
                tok_rows, head_width
            )
    else:

        def to_owner(grad):
            shares = grad.reshape(seq_count, ctx_count, seq_rows, head_width).swapaxes(0, 1)
            return lax.psum_scatter(
                shares.reshape(ctx_count * tok_rows, head_width), "ctx", scatter_dimension=0, tiled=True
            )

    attn_out_term = jnp.dot(attended_b.T, full_grads, preferred_element_type=F32)
    attn_out_grad = weight_sum(attn_out_term)
    branch_terms = jnp.dot(attended_b, attn_out_weight, preferred_element_type=F32) + jnp.dot(
        activated_b, mlp_out_weight, preferred_element_type=F32
    )
    branch_sum = line_scatter(branch_terms, "tensor")
    bias_rows = out_bias.astype(F32)
    mixed = (tokens.astype(F32) + branch_sum + bias_rows[0] + bias_rows[1]).astype(BF16)

    second_part = jnp.dot(grad_hidden, mlp_in_weight.T, preferred_element_type=F32)
    grad_proj = [
        rotate(0.125 * grad_query.reshape(tok_rows, head_width), tables, -1.0).astype(BF16),
        rotate(to_owner(grad_key), tables, -1.0).astype(BF16),
        to_owner(grad_value).astype(BF16),
    ]
    grad_proj = lax.optimization_barrier(jnp.concatenate(grad_proj, axis=1))
    qkv_term = jnp.dot(grad_proj.T, norm_first, preferred_element_type=F32)
    qkv_grad = weight_sum(qkv_term)
    flat_weight = qkv_weight.transpose(1, 0, 2).reshape(qkv_weight.shape[1], 3 * head_width)
    first_part = jnp.dot(grad_proj, flat_weight.T, preferred_element_type=F32)

    combined = first_part * gains[0] + second_part * gains[1]
    back_sum = line_scatter(combined, "tensor")
    means = small_sum(
        jnp.stack([jnp.sum(combined, axis=1), jnp.sum(combined * normed, axis=1)]), ("tensor",)
    ) * (1.0 / full_tokens.shape[1])
    own_normed = lax.dynamic_slice_in_dim(normed, column_start, local_width, 1)
    input_grad = grad_local + inverse_scale * (
        back_sum - means[0][:, None] - own_normed * means[1][:, None]
    )

    norm_term = jnp.stack(
        [
            jnp.sum(first_part * normed, axis=0),
            jnp.sum(second_part * normed, axis=0),
            jnp.sum(first_part, axis=0),
            jnp.sum(second_part, axis=0),
        ]
    )
    norm_sum = lax.dynamic_slice_in_dim(
        small_sum(norm_term, ("tensor", "ctx", "dp")), column_start, local_width, 1
    )
    bias_sum = small_sum(
        jnp.concatenate(
            [
                jnp.sum(grad_proj.astype(F32), axis=0),
                jnp.sum(grad_local, axis=0),
                jnp.sum(grad_hidden.astype(F32), axis=0),
            ]
        ),
        ("ctx", "dp"),
    )
    out_bias_grad = bias_sum[3 * head_width : 3 * head_width + local_width]
    return (
        mixed,
        input_grad,
        norm_sum[0:2],
        norm_sum[2:4],
        qkv_grad.reshape(3, head_width, -1).transpose(0, 2, 1),
        bias_sum[: 3 * head_width].reshape(3, head_width),
        attn_out_grad,
        jnp.stack([out_bias_grad, out_bias_grad]),
        mlp_in_grad,
        bias_sum[3 * head_width + local_width :],
        mlp_out_grad,
    )


def solution(mesh):
    placed = (
        P(("dp", "ctx"), "tensor"),
        P(),
        P(),
        P(),
        P(None, None, "tensor"),
        P(None, "tensor"),
        P("tensor", None),
        P(None, "tensor"),
        P(None, "tensor"),
        P("tensor"),
        P("tensor", None),
        P(("dp", "ctx"), "tensor"),
    )
    return jax.shard_map(
        local,
        mesh=mesh,
        in_specs=placed,
        out_specs=(
            P(("dp", "ctx"), "tensor"),
            P(("dp", "ctx"), "tensor"),
            P(None, "tensor"),
            P(None, "tensor"),
            P(None, None, "tensor"),
            P(None, "tensor"),
            P("tensor", None),
            P(None, "tensor"),
            P(None, "tensor"),
            P("tensor"),
            P("tensor", None),
        ),
        check_vma=False,
    )
```

time: 853 us -> 373 us (0.44)
  waiting for transfers between devices: 580 us -> 114 us
  starting transfers between devices: 0.75 us -> 121 us
  matrix products: 144 us -> 33.7 us
  Pallas kernels: 0 us -> 28.2 us
  blocking collectives: 24.6 us -> 0 us
  local copies, waits for them, and re-layouts: 53.6 us -> 39.1 us
  between operations: 14.9 us -> 2.5 us
    psum x2 -> x0, waiting for transfers between devices: 468 us -> none  [the longest x1 291 us: local(): first_full, second_full = lax.psum((first_part, second_part), 'tensor')]
    ppermute x0 -> x81, starting transfers between devices: none -> 121 us  [the longest x45 49.7 us: swap(): lax.ppermute(block, axis, [(i, i ^ bit) for i in range(lax.axis_size(axis...]
    ppermute x0 -> x81, waiting for transfers between devices: none -> 114 us  [the longest x45 48.8 us: swap(): lax.ppermute(block, axis, [(i, i ^ bit) for i in range(lax.axis_size(axis...]
    dot_general x18 -> x14, matrix products: 144 us -> 33.7 us  [the longest x1 5.71 us: local(): first_part = jnp.dot(grad_proj, flat_weight.T, preferred_element_type=F32)]
    all_gather x4 -> x0, waiting for transfers between devices: 83.9 us -> none  [the longest x1 45.9 us: local(): lax.all_gather(tokens, 'tensor', axis=1, tiled=True)]
    pallas_call x0 -> x1, Pallas kernels: none -> 28.2 us  [attention(): pl.pallas_call(functools.partial(attention_body, heads, chunk), grid=(seq...]
    reduce_scatter x2 -> x0, waiting for transfers between devices: 27.1 us -> none  [the longest x1 27.1 us: local(): lax.psum_scatter(branch_terms, 'tensor', scatter_dimension=1, tiled=True)]
    psum x1 -> x0, blocking collectives: 24.6 us -> none  [local(): lax.psum((qkv_term, qkv_bias_term, attn_out_term, out_bias_term, mlp_in_t...]
  transfers between devices with their start and end apart: 8 -> 81, of which waited for: 6 -> 31; matrix products, arithmetic and copies ran while one was open for 13% -> 25% of each run, Pallas kernels for 0% -> 8%
where the time goes in v1:
time: 373 us; the launch traced here: 371 us
  starting transfers between devices  121 us (32%)
  waiting for transfers between devices  114 us (31%)
  local copies, waits for them, and re-layouts  39.1 us (10%)
  matrix products  33.7 us (9%)
  other arithmetic  33.2 us (9%)
  Pallas kernels  28.2 us (8%)
    ppermute x45, starting transfers between devices, swap(): lax.ppermute(block, axis, [(i, i ^ bit) for i in range(lax.axis_size(axis...  49.7 us
    ppermute x45, waiting for transfers between devices, swap(): lax.ppermute(block, axis, [(i, i ^ bit) for i in range(lax.axis_size(axis...  48.8 us
    ppermute x12, waiting for transfers between devices, line_gather(): lax.ppermute(falling, axis, [(i + 1, i) for i in range(size - 1 - step)])  30.7 us
    ppermute x12, starting transfers between devices, line_gather(): lax.ppermute(rising, axis, [(i, i + 1) for i in range(step, size - 1)])  28.3 us
    pallas_call x1, Pallas kernels, attention(): pl.pallas_call(functools.partial(attention_body, heads, chunk), grid=(seq...  28.2 us
    unnamed x106, local copies, waits for them, and re-layouts  25.2 us
    ppermute x6, starting transfers between devices, line_scatter(): lax.ppermute(up.astype(BF16), axis, [(i, i + 1) for i in range(size - 1)...  21.2 us
    ppermute x6, waiting for transfers between devices, line_scatter(): lax.ppermute(up.astype(BF16), axis, [(i, i + 1) for i in range(size - 1)...  18.4 us
  transfers between devices with their start and end apart: 81, of which 31 were waited for; matrix products, arithmetic and copies ran while one was open for 25% of the time, Pallas kernels for 8%

profile of v1, /device:TPU:0, one launch (start us, length us, event | category | flops | bytes accessed | tf_op | source)
XLA Modules:
  0.0 370.8 jit_solution(15635804953148675648)
XLA Ops:
  0.7 2.0 fusion.94
  4.0 6.3 %collective-permute-start = (bf16[512,256]{1,0:T(8,128)(2,1)}, bf16[512,256]{1,0:T(8,128)(2,1)}, u32[]{:S(2)}, u32[]{:S(2)}) collective-permute-start(bf16[512,256]{1,0:T(8,128)(2,1)} %get-tuple-element.131), channel_id=1, source_target_pairs={{0,1},{1,2},{2,3},{4,5},{5,6},{6,7},{8,9},{9,10},{10,11},{12,13},{... | collective-permute-start | bytes 786440 | tf_op jit(solution)/shard_map/ppermute | solution.py:27
  11.5 5.3 %collective-permute-start.6 = (bf16[512,256]{1,0:T(8,128)(2,1)}, bf16[512,256]{1,0:T(8,128)(2,1)}, u32[]{:S(2)}, u32[]{:S(2)}) collective-permute-start(bf16[512,256]{1,0:T(8,128)(2,1)} %get-tuple-element.132), channel_id=1, source_target_pairs={{0,1},{1,2},{2,3},{4,5},{5,6},{6,7},{8,9},{9,10},{10,11},{12,13},{... | collective-permute-start | bytes 786440 | tf_op jit(solution)/shard_map/ppermute | solution.py:27
  17.8 5.6 %fusion.9 = (f32[1024,256]{1,0:T(8,128)S(1)}, f32[1024,256]{1,0:T(8,128)}, f32[1024,256]{1,0:T(8,128)}) fusion(f32[256]{0:T(256)S(1)} %fusion.65, f32[1024]{0:T(1024)S(1)} %bitcast.276, pred[256]{0:T(512)(128)(4,1)S(1)} %get-tuple-element.157, pred[256]{0:T(512)(128)(4,1)S(1)} %get-tuple-element.158, pred[256]{0:T(512)(128)(4,1)S(1)} %broadcast_compare_fusion.1), kind=kLoop, calls=%fused_computation.43 | loop fusion | flops 1048576 | bytes 3151616 | tf_op jit(solution)/shard_map/jit(_where)/select_n | solution.py:225
  31.5 2.6 copy.31
  34.2 2.0 collective-permute-done.4
  38.2 4.9 %collective-permute-done.10 = bf16[512,256]{1,0:T(8,128)(2,1)} collective-permute-done((bf16[512,256]{1,0:T(8,128)(2,1)}, bf16[512,256]{1,0:T(8,128)(2,1)}, u32[]{:S(2)}, u32[]{:S(2)}) %collective-permute-start.10) | collective-permute-done | bytes 262176 | tf_op jit(solution)/shard_map/ppermute | solution.py:28
  52.5 2.6 collective-permute-done.11
  57.7 4.6 %collective-permute-start.12 = (bf16[512,256]{1,0:T(8,128)(2,1)S(1)}, bf16[512,256]{1,0:T(8,128)(2,1)S(1)}, u32[]{:S(2)}, u32[]{:S(2)}) collective-permute-start(bf16[512,256]{1,0:T(8,128)(2,1)S(1)} %get-tuple-element.127), channel_id=1, source_target_pairs={{0,1},{1,2},{2,3},{4,5},{5,6},{6,7},{8,9},{9,10},{10,11},{12,13},{... | collective-permute-start | bytes 786440 | tf_op jit(solution)/shard_map/ppermute | solution.py:27
  63.5 4.7 %collective-permute-start.18 = (bf16[512,256]{1,0:T(8,128)(2,1)S(1)}, bf16[512,256]{1,0:T(8,128)(2,1)S(1)}, u32[]{:S(2)}, u32[]{:S(2)}) collective-permute-start(bf16[512,256]{1,0:T(8,128)(2,1)S(1)} %get-tuple-element.128), channel_id=1, source_target_pairs={{0,1},{1,2},{2,3},{4,5},{5,6},{6,7},{8,9},{9,10},{10,11},{12,13},{... | collective-permute-start | bytes 786440 | tf_op jit(solution)/shard_map/ppermute | solution.py:27
  75.2 3.7 fusion.6
  78.9 4.4 %fusion.100 = f32[1024,1024]{1,0:T(8,128)} fusion(bf16[1024,1024]{1,0:T(8,128)(2,1)S(1)} %get-tuple-element.28, bf16[1024,1024]{1,0:T(8,128)(2,1)S(1)} %copy-done.38), kind=kOutput, calls=%fused_computation.264 | convolution fusion | flops 2147483648 | bytes 8388608 | tf_op jit(solution)/shard_map/dot_general | solution.py:342
  89.1 8.6 %collective-permute-done.16 = bf16[512,256]{1,0:T(8,128)(2,1)S(1)} collective-permute-done((bf16[512,256]{1,0:T(8,128)(2,1)S(1)}, bf16[512,256]{1,0:T(8,128)(2,1)S(1)}, u32[]{:S(2)}, u32[]{:S(2)}) %collective-permute-start.16) | collective-permute-done | bytes 262176 | tf_op jit(solution)/shard_map/ppermute | solution.py:28
  99.7 4.2 %collective-permute-done.22 = bf16[512,256]{1,0:T(8,128)(2,1)S(1)} collective-permute-done((bf16[512,256]{1,0:T(8,128)(2,1)S(1)}, bf16[512,256]{1,0:T(8,128)(2,1)S(1)}, u32[]{:S(2)}, u32[]{:S(2)}) %collective-permute-start.22) | collective-permute-done | bytes 262176 | tf_op jit(solution)/shard_map/ppermute | solution.py:28
  103.9 1.7 collective-permute-start.23
  105.9 3.6 collective-permute-done.17
  109.7 4.7 %collective-permute-done.23 = bf16[512,256]{1,0:T(8,128)(2,1)S(1)} collective-permute-done((bf16[512,256]{1,0:T(8,128)(2,1)S(1)}, bf16[512,256]{1,0:T(8,128)(2,1)S(1)}, u32[]{:S(2)}, u32[]{:S(2)}) %collective-permute-start.23) | collective-permute-done | bytes 262176 | tf_op jit(solution)/shard_map/ppermute | solution.py:28
  114.5 2.4 fusion.71
  117.0 2.4 multiply_convert_fusion
  120.6 2.7 fusion.73
  126.4 4.4 %fusion.101 = f32[1024,1024]{1,0:T(8,128)} fusion(bf16[1024,1024]{1,0:T(8,128)(2,1)S(1)} %multiply_convert_fusion, bf16[1024,1024]{1,0:T(8,128)(2,1)S(1)} %copy-done), kind=kOutput, calls=%fused_computation.265 | convolution fusion | flops 2147483648 | bytes 8388608 | tf_op jit(solution)/shard_map/dot_general | solution.py:349
  131.8 28.2 %shard_map.203 = (bf16[1,1024,256]{2,1,0:T(8,128)(2,1)S(1)}, f32[1,1024,256]{2,1,0:T(8,128)S(1)}, f32[1,2048,256]{2,1,0:T(8,128)S(1)}, f32[1,2048,256]{2,1,0:T(8,128)S(1)}) custom-call(s32[2]{0:T(128)S(1)} %get-tuple-element.156.qmax, s32[4]{0:T(128)S(1)} %get-tuple-element.153.kmin, bf16[1,1024,256]{2,1,0:T(8,128)(2,1)S(1)} %multiply_bitcast_fusion.1.q, ...), custom_call_target="tpu_custom_call" | custom-call | flops 25769803776 | bytes 8388608 | tf_op jit(solution)/shard_map/pallas_call | solution.py:175
  162.2 2.1 copy.32
  164.3 2.5 fusion.7
  166.9 12.1 %collective-permute-start.57 = (bf16[4,32,1024]{2,1,0:T(8,128)(2,1)S(1)}, bf16[4,32,1024]{2,1,0:T(8,128)(2,1)S(1)}, u32[]{:S(2)}, u32[]{:S(2)}) collective-permute-start(bf16[4,32,1024]{2,1,0:T(8,128)(2,1)S(1)} %fusion.54), channel_id=1, source_target_pairs={{0,4},{4,0},{1,5},{5,1},{2,6},{6,2},{3,7},{7,3},{8,12},{12,8},{9,1... | collective-permute-start | bytes 786440 | tf_op jit(solution)/shard_map/ppermute | solution.py:65
  180.2 1.6 collective-permute-start.58
  181.8 1.5 collective-permute-start.60
  184.6 2.5 collective-permute-done.60
  188.3 1.4 collective-permute-start.61
  190.7 1.5 collective-permute-start.25
  192.9 1.5 collective-permute-start.63
  194.4 2.6 collective-permute-done.62
  199.9 3.2 collective-permute-done.25
  203.4 1.8 fusion.77
  206.2 1.5 collective-permute-start.76
  208.9 1.8 fusion.79
  211.6 3.1 collective-permute-done.74
  215.2 5.4 %collective-permute-done.76 = bf16[128,1024]{1,0:T(8,128)(2,1)S(1)} collective-permute-done((bf16[128,1024]{1,0:T(8,128)(2,1)S(1)}, bf16[128,1024]{1,0:T(8,128)(2,1)S(1)}, u32[]{:S(2)}, u32[]{:S(2)}) %collective-permute-start.76) | collective-permute-done | bytes 262176 | tf_op jit(solution)/shard_map/ppermute | solution.py:65
  223.9 2.0 collective-permute-done.66
  226.6 3.1 collective-permute-done.68
  229.7 5.2 %collective-permute-start.26 = (bf16[1024,256]{1,0:T(8,128)(2,1)S(1)}, bf16[1024,256]{1,0:T(8,128)(2,1)}, u32[]{:S(2)}, u32[]{:S(2)}) collective-permute-start(bf16[1024,256]{1,0:T(8,128)(2,1)S(1)} %add_convert_fusion.11), channel_id=1, source_target_pairs={{0,1},{1,2},{4,5},{5,6},{8,9},{9,10},{12,13},{13,14},{16,17},{17,1... | collective-permute-start | bytes 1572872 | tf_op jit(solution)/shard_map/ppermute | solution.py:52
  241.3 1.6 collective-permute-start.79
  245.1 5.7 %fusion.75 = (f32[1024]{0:T(1024)S(1)}, f32[1024]{0:T(1024)S(1)}, f32[1024]{0:T(1024)S(1)}, f32[1024]{0:T(1024)S(1)}, f32[1024]{0:T(1024)S(1)}, /*index=5*/f32[1...) fusion(f32[1024]{0:T(1024)S(1)} %add_rsqrt_fusion, f32[1024]{0:T(1024)S(1)} %broadcast_multiply_fusion, ...), kind=kOutput, calls=%fused_computation.244 | convolution fusion | flops 1626335232 | bytes 17866752 | tf_op jit(solution)/shard_map/dot_general | solution.py:359
  250.9 1.8 fusion.102
  252.8 2.0 collective-permute-start.41
  256.9 3.0 collective-permute-start.40
  259.8 1.6 collective-permute-done.42
  264.8 2.7 collective-permute-done.44
  268.6 2.9 collective-permute-done.45
  272.9 1.6 collective-permute-start.71
  275.3 5.4 %collective-permute-done.69 = bf16[128,1024]{1,0:T(8,128)(2,1)S(1)} collective-permute-done((bf16[128,1024]{1,0:T(8,128)(2,1)S(1)}, bf16[128,1024]{1,0:T(8,128)(2,1)S(1)}, u32[]{:S(2)}, u32[]{:S(2)}) %collective-permute-start.69) | collective-permute-done | bytes 262176 | tf_op jit(solution)/shard_map/ppermute | solution.py:65
  280.7 3.8 %collective-permute-start.27 = (bf16[1024,256]{1,0:T(8,128)(2,1)S(1)}, bf16[1024,256]{1,0:T(8,128)(2,1)S(1)}, u32[]{:S(2)}, u32[]{:S(2)}) collective-permute-start(bf16[1024,256]{1,0:T(8,128)(2,1)S(1)} %get-tuple-element.79), channel_id=1, source_target_pairs={{0,1},{1,2},{2,3},{4,5},{5,6},{6,7},{8,9},{9,10},{10,11},{12,13},{... | collective-permute-start | bytes 1572872 | tf_op jit(solution)/shard_map/ppermute | solution.py:52
  284.5 1.9 collective-permute-start.33
  289.3 14.4 %collective-permute-done.33 = bf16[1024,256]{1,0:T(8,128)(2,1)S(1)} collective-permute-done((bf16[1024,256]{1,0:T(8,128)(2,1)S(1)}, bf16[1024,256]{1,0:T(8,128)(2,1)S(1)}, u32[]{:S(2)}, u32[]{:S(2)}) %collective-permute-start.33) | collective-permute-done | bytes 524320 | tf_op jit(solution)/shard_map/ppermute | solution.py:52
  306.1 4.4 %collective-permute-start.34 = (bf16[1024,256]{1,0:T(8,128)(2,1)S(1)}, bf16[1024,256]{1,0:T(8,128)(2,1)S(1)}, u32[]{:S(2)}, u32[]{:S(2)}) collective-permute-start(bf16[1024,256]{1,0:T(8,128)(2,1)S(1)} %add_convert_fusion.5), channel_id=1, source_target_pairs={{0,1},{1,2},{4,5},{5,6},{8,9},{9,10},{12,13},{13,14},{16,17},{17,1... | collective-permute-start | bytes 1572872 | tf_op jit(solution)/shard_map/ppermute | solution.py:52
  311.5 4.8 %collective-permute-done.48 = bf16[96,1024]{1,0:T(8,128)(2,1)S(1)} collective-permute-done((bf16[96,1024]{1,0:T(8,128)(2,1)S(1)}, bf16[96,1024]{1,0:T(8,128)(2,1)S(1)}, u32[]{:S(2)}, u32[]{:S(2)}) %collective-permute-start.48) | collective-permute-done | bytes 196640 | tf_op jit(solution)/shard_map/ppermute | solution.py:65
  322.1 4.7 %collective-permute-done.50 = bf16[96,1024]{1,0:T(8,128)(2,1)S(1)} collective-permute-done((bf16[96,1024]{1,0:T(8,128)(2,1)S(1)}, bf16[96,1024]{1,0:T(8,128)(2,1)S(1)}, u32[]{:S(2)}, u32[]{:S(2)}) %collective-permute-start.50) | collective-permute-done | bytes 196640 | tf_op jit(solution)/shard_map/ppermute | solution.py:65
  326.9 4.4 %collective-permute-start.35 = (bf16[1024,256]{1,0:T(8,128)(2,1)S(1)}, bf16[1024,256]{1,0:T(8,128)(2,1)S(1)}, u32[]{:S(2)}, u32[]{:S(2)}) collective-permute-start(bf16[1024,256]{1,0:T(8,128)(2,1)S(1)} %get-tuple-element.75), channel_id=1, source_target_pairs={{0,1},{1,2},{2,3},{4,5},{5,6},{6,7},{8,9},{9,10},{10,11},{12,13},{... | collective-permute-start | bytes 1572872 | tf_op jit(solution)/shard_map/ppermute | solution.py:52
  334.8 4.7 %bitcast_convert_fusion = (f32[1024,1024]{1,0:T(8,128)}, f32[1024,1024]{1,0:T(8,128)}) fusion(bf16[2,4,128,1024]{3,2,1,0:T(8,128)(2,1)S(1)} %pad_maximum_fusion.3, bf16[2,4,128,1024]{3,2,1,0:T(8,128)(2,1)S(1)} %pad_maximum_fusion.2), kind=kLoop, calls=%fused_computation.29 | loop fusion | flops 2097152 | bytes 12582912 | tf_op jit(solution)/shard_map/convert_element_type | solution.py:99
  340.3 15.6 %collective-permute-done.38 = bf16[1024,256]{1,0:T(8,128)(2,1)S(1)} collective-permute-done((bf16[1024,256]{1,0:T(8,128)(2,1)S(1)}, bf16[1024,256]{1,0:T(8,128)(2,1)S(1)}, u32[]{:S(2)}, u32[]{:S(2)}) %collective-permute-start.38) | collective-permute-done | bytes 524320 | tf_op jit(solution)/shard_map/ppermute | solution.py:55
  355.9 1.5 convert_reduce_fusion.3
  359.7 2.6 collective-permute-done.55
  363.2 2.0 convert_bitcast_fusion
  365.3 3.5 copy.33
  (345 shorter events, 103.9 us)
Async XLA Ops:
  2.7 22.4 %collective-permute-start.3 = (bf16[512,256]{1,0:T(8,128)(2,1)}, bf16[512,256]{1,0:T(8,128)(2,1)S(1)}, u32[]{:S(2)}, u32[]{:S(2)}) collective-permute-start(bf16[512,256]{1,0:T(8,128)(2,1)} %get-tuple-element.131), channel_id=1, source_target_pairs={{1,0},{2,1},{3,2},{5,4},{6,5},{7,6},{9,8},{10,9},{11,10},{13,12},{... | collective-permute-start | bytes 786440 | tf_op jit(solution)/shard_map/ppermute | solution.py:28
  4.0 22.4 %collective-permute-start = (bf16[512,256]{1,0:T(8,128)(2,1)}, bf16[512,256]{1,0:T(8,128)(2,1)}, u32[]{:S(2)}, u32[]{:S(2)}) collective-permute-start(bf16[512,256]{1,0:T(8,128)(2,1)} %get-tuple-element.131), channel_id=1, source_target_pairs={{0,1},{1,2},{2,3},{4,5},{5,6},{6,7},{8,9},{9,10},{10,11},{12,13},{... | collective-permute-start | bytes 786440 | tf_op jit(solution)/shard_map/ppermute | solution.py:27
  10.3 17.5 %collective-permute-start.9 = (bf16[512,256]{1,0:T(8,128)(2,1)}, bf16[512,256]{1,0:T(8,128)(2,1)}, u32[]{:S(2)}, u32[]{:S(2)}) collective-permute-start(bf16[512,256]{1,0:T(8,128)(2,1)} %get-tuple-element.132), channel_id=1, source_target_pairs={{1,0},{2,1},{3,2},{5,4},{6,5},{7,6},{9,8},{10,9},{11,10},{13,12},{... | collective-permute-start | bytes 786440 | tf_op jit(solution)/shard_map/ppermute | solution.py:28
  11.5 12.1 %collective-permute-start.6 = (bf16[512,256]{1,0:T(8,128)(2,1)}, bf16[512,256]{1,0:T(8,128)(2,1)}, u32[]{:S(2)}, u32[]{:S(2)}) collective-permute-start(bf16[512,256]{1,0:T(8,128)(2,1)} %get-tuple-element.132), channel_id=1, source_target_pairs={{0,1},{1,2},{2,3},{4,5},{5,6},{6,7},{8,9},{9,10},{10,11},{12,13},{... | collective-permute-start | bytes 786440 | tf_op jit(solution)/shard_map/ppermute | solution.py:27
  23.7 5.4 %collective-permute-start.7 = (bf16[512,256]{1,0:T(8,128)(2,1)}, bf16[512,256]{1,0:T(8,128)(2,1)}, u32[]{:S(2)}, u32[]{:S(2)}) collective-permute-start(bf16[512,256]{1,0:T(8,128)(2,1)} %collective-permute-done.6), channel_id=1, source_target_pairs={{1,2},{2,3},{5,6},{6,7},{9,10},{10,11},{13,14},{14,15},{17,18},{18... | collective-permute-start | bytes 786440 | tf_op jit(solution)/shard_map/ppermute | solution.py:27
  25.1 11.1 %collective-permute-start.4 = (bf16[512,256]{1,0:T(8,128)(2,1)S(1)}, bf16[512,256]{1,0:T(8,128)(2,1)}, u32[]{:S(2)}, u32[]{:S(2)}) collective-permute-start(bf16[512,256]{1,0:T(8,128)(2,1)S(1)} %collective-permute-done.3), channel_id=1, source_target_pairs={{1,0},{2,1},{5,4},{6,5},{9,8},{10,9},{13,12},{14,13},{17,16},{18,1... | collective-permute-start | bytes 786440 | tf_op jit(solution)/shard_map/ppermute | solution.py:28
  26.4 11.1 %collective-permute-start.1 = (bf16[512,256]{1,0:T(8,128)(2,1)}, bf16[512,256]{1,0:T(8,128)(2,1)}, u32[]{:S(2)}, u32[]{:S(2)}) collective-permute-start(bf16[512,256]{1,0:T(8,128)(2,1)} %collective-permute-done), channel_id=1, source_target_pairs={{1,2},{2,3},{5,6},{6,7},{9,10},{10,11},{13,14},{14,15},{17,18},{18... | collective-permute-start | bytes 786440 | tf_op jit(solution)/shard_map/ppermute | solution.py:27
  27.8 15.3 %collective-permute-start.10 = (bf16[512,256]{1,0:T(8,128)(2,1)}, bf16[512,256]{1,0:T(8,128)(2,1)}, u32[]{:S(2)}, u32[]{:S(2)}) collective-permute-start(bf16[512,256]{1,0:T(8,128)(2,1)} %collective-permute-done.9), channel_id=1, source_target_pairs={{1,0},{2,1},{5,4},{6,5},{9,8},{10,9},{13,12},{14,13},{17,16},{18,1... | collective-permute-start | bytes 786440 | tf_op jit(solution)/shard_map/ppermute | solution.py:28
  29.1 15.3 %collective-permute-start.8 = (bf16[512,256]{1,0:T(8,128)(2,1)}, bf16[512,256]{1,0:T(8,128)(2,1)}, u32[]{:S(2)}, u32[]{:S(2)}) collective-permute-start(bf16[512,256]{1,0:T(8,128)(2,1)} %collective-permute-done.7), channel_id=1, source_target_pairs={{2,3},{6,7},{10,11},{14,15},{18,19},{22,23},{26,27},{30,31}} | collective-permute-start | bytes 786440 | tf_op jit(solution)/shard_map/ppermute | solution.py:27
  36.2 16.1 %collective-permute-start.5 = (bf16[512,256]{1,0:T(8,128)(2,1)}, bf16[512,256]{1,0:T(8,128)(2,1)S(1)}, u32[]{:S(2)}, u32[]{:S(2)}) collective-permute-start(bf16[512,256]{1,0:T(8,128)(2,1)} %collective-permute-done.4), channel_id=1, source_target_pairs={{1,0},{5,4},{9,8},{13,12},{17,16},{21,20},{25,24},{29,28}} | collective-permute-start | bytes 786440 | tf_op jit(solution)/shard_map/ppermute | solution.py:28
  37.5 9.8 %collective-permute-start.2 = (bf16[512,256]{1,0:T(8,128)(2,1)}, bf16[512,256]{1,0:T(8,128)(2,1)S(1)}, u32[]{:S(2)}, u32[]{:S(2)}) collective-permute-start(bf16[512,256]{1,0:T(8,128)(2,1)} %collective-permute-done.1), channel_id=1, source_target_pairs={{2,3},{6,7},{10,11},{14,15},{18,19},{22,23},{26,27},{30,31}} | collective-permute-start | bytes 786440 | tf_op jit(solution)/shard_map/ppermute | solution.py:27
  43.1 12.0 %collective-permute-start.11 = (bf16[512,256]{1,0:T(8,128)(2,1)}, bf16[512,256]{1,0:T(8,128)(2,1)S(1)}, u32[]{:S(2)}, u32[]{:S(2)}) collective-permute-start(bf16[512,256]{1,0:T(8,128)(2,1)} %collective-permute-done.10), channel_id=1, source_target_pairs={{1,0},{5,4},{9,8},{13,12},{17,16},{21,20},{25,24},{29,28}} | collective-permute-start | bytes 786440 | tf_op jit(solution)/shard_map/ppermute | solution.py:28
  56.4 28.1 %collective-permute-start.15 = (bf16[512,256]{1,0:T(8,128)(2,1)S(1)}, bf16[512,256]{1,0:T(8,128)(2,1)S(1)}, u32[]{:S(2)}, u32[]{:S(2)}) collective-permute-start(bf16[512,256]{1,0:T(8,128)(2,1)S(1)} %get-tuple-element.127), channel_id=1, source_target_pairs={{1,0},{2,1},{3,2},{5,4},{6,5},{7,6},{9,8},{10,9},{11,10},{13,12},{... | collective-permute-start | bytes 786440 | tf_op jit(solution)/shard_map/ppermute | solution.py:28
  57.7 28.1 %collective-permute-start.12 = (bf16[512,256]{1,0:T(8,128)(2,1)S(1)}, bf16[512,256]{1,0:T(8,128)(2,1)S(1)}, u32[]{:S(2)}, u32[]{:S(2)}) collective-permute-start(bf16[512,256]{1,0:T(8,128)(2,1)S(1)} %get-tuple-element.127), channel_id=1, source_target_pairs={{0,1},{1,2},{2,3},{4,5},{5,6},{6,7},{8,9},{9,10},{10,11},{12,13},{... | collective-permute-start | bytes 786440 | tf_op jit(solution)/shard_map/ppermute | solution.py:27
  62.2 24.2 %collective-permute-start.21 = (bf16[512,256]{1,0:T(8,128)(2,1)S(1)}, bf16[512,256]{1,0:T(8,128)(2,1)S(1)}, u32[]{:S(2)}, u32[]{:S(2)}) collective-permute-start(bf16[512,256]{1,0:T(8,128)(2,1)S(1)} %get-tuple-element.128), channel_id=1, source_target_pairs={{1,0},{2,1},{3,2},{5,4},{6,5},{7,6},{9,8},{10,9},{11,10},{13,12},{... | collective-permute-start | bytes 786440 | tf_op jit(solution)/shard_map/ppermute | solution.py:28
  63.5 20.0 %collective-permute-start.18 = (bf16[512,256]{1,0:T(8,128)(2,1)S(1)}, bf16[512,256]{1,0:T(8,128)(2,1)S(1)}, u32[]{:S(2)}, u32[]{:S(2)}) collective-permute-start(bf16[512,256]{1,0:T(8,128)(2,1)S(1)} %get-tuple-element.128), channel_id=1, source_target_pairs={{0,1},{1,2},{2,3},{4,5},{5,6},{6,7},{8,9},{9,10},{10,11},{12,13},{... | collective-permute-start | bytes 786440 | tf_op jit(solution)/shard_map/ppermute | solution.py:27
  75.1 55.7 %collective-permute-start.24 = (bf16[2,1024,256]{2,1,0:T(8,128)(2,1)S(1)}, bf16[2,1024,256]{2,1,0:T(8,128)(2,1)S(1)}, u32[]{:S(2)}, u32[]{:S(2)}) collective-permute-start(bf16[2,1024,256]{2,1,0:T(8,128)(2,1)S(1)} %get-tuple-element.108), channel_id=1, source_target_pairs={{0,4},{4,0},{1,5},{5,1},{2,6},{6,2},{3,7},{7,3},{8,12},{12,8},{9,1... | collective-permute-start | bytes 3145736 | tf_op jit(solution)/shard_map/ppermute | solution.py:65
  84.5 13.2 %collective-permute-start.16 = (bf16[512,256]{1,0:T(8,128)(2,1)S(1)}, bf16[512,256]{1,0:T(8,128)(2,1)S(1)}, u32[]{:S(2)}, u32[]{:S(2)}) collective-permute-start(bf16[512,256]{1,0:T(8,128)(2,1)S(1)} %collective-permute-done.15), channel_id=1, source_target_pairs={{1,0},{2,1},{5,4},{6,5},{9,8},{10,9},{13,12},{14,13},{17,16},{18,1... | collective-permute-start | bytes 786440 | tf_op jit(solution)/shard_map/ppermute | solution.py:28
  85.8 13.2 %collective-permute-start.13 = (bf16[512,256]{1,0:T(8,128)(2,1)S(1)}, bf16[512,256]{1,0:T(8,128)(2,1)S(1)}, u32[]{:S(2)}, u32[]{:S(2)}) collective-permute-start(bf16[512,256]{1,0:T(8,128)(2,1)S(1)} %collective-permute-done.12), channel_id=1, source_target_pairs={{1,2},{2,3},{5,6},{6,7},{9,10},{10,11},{13,14},{14,15},{17,18},{18... | collective-permute-start | bytes 786440 | tf_op jit(solution)/shard_map/ppermute | solution.py:27
  86.5 17.4 %collective-permute-start.22 = (bf16[512,256]{1,0:T(8,128)(2,1)S(1)}, bf16[512,256]{1,0:T(8,128)(2,1)S(1)}, u32[]{:S(2)}, u32[]{:S(2)}) collective-permute-start(bf16[512,256]{1,0:T(8,128)(2,1)S(1)} %collective-permute-done.21), channel_id=1, source_target_pairs={{1,0},{2,1},{5,4},{6,5},{9,8},{10,9},{13,12},{14,13},{17,16},{18,1... | collective-permute-start | bytes 786440 | tf_op jit(solution)/shard_map/ppermute | solution.py:28
  87.8 17.8 %collective-permute-start.20 = (bf16[512,256]{1,0:T(8,128)(2,1)S(1)}, bf16[512,256]{1,0:T(8,128)(2,1)S(1)}, u32[]{:S(2)}, u32[]{:S(2)}) collective-permute-start(bf16[512,256]{1,0:T(8,128)(2,1)S(1)} %collective-permute-done.19), channel_id=1, source_target_pairs={{2,3},{6,7},{10,11},{14,15},{18,19},{22,23},{26,27},{30,31}} | collective-permute-start | bytes 786440 | tf_op jit(solution)/shard_map/ppermute | solution.py:27
  97.7 11.8 %collective-permute-start.17 = (bf16[512,256]{1,0:T(8,128)(2,1)S(1)}, bf16[512,256]{1,0:T(8,128)(2,1)S(1)}, u32[]{:S(2)}, u32[]{:S(2)}) collective-permute-start(bf16[512,256]{1,0:T(8,128)(2,1)S(1)} %collective-permute-done.16), channel_id=1, source_target_pairs={{1,0},{5,4},{9,8},{13,12},{17,16},{21,20},{25,24},{29,28}} | collective-permute-start | bytes 786440 | tf_op jit(solution)/shard_map/ppermute | solution.py:28
  99.0 6.7 %collective-permute-start.14 = (bf16[512,256]{1,0:T(8,128)(2,1)S(1)}, bf16[512,256]{1,0:T(8,128)(2,1)S(1)}, u32[]{:S(2)}, u32[]{:S(2)}) collective-permute-start(bf16[512,256]{1,0:T(8,128)(2,1)S(1)} %collective-permute-done.13), channel_id=1, source_target_pairs={{2,3},{6,7},{10,11},{14,15},{18,19},{22,23},{26,27},{30,31}} | collective-permute-start | bytes 786440 | tf_op jit(solution)/shard_map/ppermute | solution.py:27
  103.9 10.5 %collective-permute-start.23 = (bf16[512,256]{1,0:T(8,128)(2,1)S(1)}, bf16[512,256]{1,0:T(8,128)(2,1)S(1)}, u32[]{:S(2)}, u32[]{:S(2)}) collective-permute-start(bf16[512,256]{1,0:T(8,128)(2,1)S(1)} %collective-permute-done.22), channel_id=1, source_target_pairs={{1,0},{5,4},{9,8},{13,12},{17,16},{21,20},{25,24},{29,28}} | collective-permute-start | bytes 786440 | tf_op jit(solution)/shard_map/ppermute | solution.py:28
  120.6 82.8 %collective-permute-start.73 = (bf16[4,128,1024]{2,1,0:T(8,128)(2,1)}, bf16[4,128,1024]{2,1,0:T(8,128)(2,1)}, u32[]{:S(2)}, u32[]{:S(2)}) collective-permute-start(bf16[4,128,1024]{2,1,0:T(8,128)(2,1)} %fusion.15), channel_id=1, source_target_pairs={{0,4},{4,0},{1,5},{5,1},{2,6},{6,2},{3,7},{7,3},{8,12},{12,8},{9,1... | collective-permute-start | bytes 3145736 | tf_op jit(solution)/shard_map/ppermute | solution.py:65
  124.5 84.4 %collective-permute-start.65 = (bf16[4,128,1024]{2,1,0:T(8,128)(2,1)}, bf16[4,128,1024]{2,1,0:T(8,128)(2,1)}, u32[]{:S(2)}, u32[]{:S(2)}) collective-permute-start(bf16[4,128,1024]{2,1,0:T(8,128)(2,1)} %fusion.14), channel_id=1, source_target_pairs={{0,4},{4,0},{1,5},{5,1},{2,6},{6,2},{3,7},{7,3},{8,12},{12,8},{9,1... | collective-permute-start | bytes 3145736 | tf_op jit(solution)/shard_map/ppermute | solution.py:65
  166.9 13.2 %collective-permute-start.57 = (bf16[4,32,1024]{2,1,0:T(8,128)(2,1)S(1)}, bf16[4,32,1024]{2,1,0:T(8,128)(2,1)S(1)}, u32[]{:S(2)}, u32[]{:S(2)}) collective-permute-start(bf16[4,32,1024]{2,1,0:T(8,128)(2,1)S(1)} %fusion.54), channel_id=1, source_target_pairs={{0,4},{4,0},{1,5},{5,1},{2,6},{6,2},{3,7},{7,3},{8,12},{12,8},{9,1... | collective-permute-start | bytes 786440 | tf_op jit(solution)/shard_map/ppermute | solution.py:65
  190.7 12.4 %collective-permute-start.25 = (bf16[1024,256]{1,0:T(8,128)(2,1)S(1)}, bf16[1024,256]{1,0:T(8,128)(2,1)S(1)}, u32[]{:S(2)}, u32[]{:S(2)}) collective-permute-start(bf16[1024,256]{1,0:T(8,128)(2,1)S(1)} %get-tuple-element.81), channel_id=1, source_target_pairs={{0,1},{4,5},{8,9},{12,13},{16,17},{20,21},{24,25},{28,29}} | collective-permute-start | bytes 1572872 | tf_op jit(solution)/shard_map/ppermute | solution.py:52
  199.8 37.2 %collective-permute-start.31 = (f32[1,1024,256]{2,1,0:T(8,128)S(1)}, f32[1,1024,256]{2,1,0:T(8,128)S(1)}, u32[]{:S(2)}, u32[]{:S(2)}) collective-permute-start(f32[1,1024,256]{2,1,0:T(8,128)S(1)} %slice.182), channel_id=1, source_target_pairs={{0,4},{4,0},{1,5},{5,1},{2,6},{6,2},{3,7},{7,3},{8,12},{12,8},{9,1... | collective-permute-start | bytes 3145736 | tf_op jit(solution)/shard_map/ppermute | solution.py:65
  205.3 9.3 %collective-permute-start.74 = (bf16[128,1024]{1,0:T(8,128)(2,1)S(1)}, bf16[128,1024]{1,0:T(8,128)(2,1)S(1)}, u32[]{:S(2)}, u32[]{:S(2)}) collective-permute-start(bf16[128,1024]{1,0:T(8,128)(2,1)S(1)} %get-tuple-element.94), channel_id=1, source_target_pairs={{0,8},{8,0},{16,24},{24,16},{1,9},{9,1},{17,25},{25,17},{2,10},{10... | collective-permute-start | bytes 786440 | tf_op jit(solution)/shard_map/ppermute | solution.py:65
  206.2 14.4 %collective-permute-start.76 = (bf16[128,1024]{1,0:T(8,128)(2,1)S(1)}, bf16[128,1024]{1,0:T(8,128)(2,1)S(1)}, u32[]{:S(2)}, u32[]{:S(2)}) collective-permute-start(bf16[128,1024]{1,0:T(8,128)(2,1)S(1)} %get-tuple-element.95), channel_id=1, source_target_pairs={{0,24},{8,16},{16,8},{24,0},{1,25},{9,17},{17,9},{25,1},{2,26},{10... | collective-permute-start | bytes 786440 | tf_op jit(solution)/shard_map/ppermute | solution.py:65
  207.7 15.2 %collective-permute-start.75 = (bf16[128,1024]{1,0:T(8,128)(2,1)S(1)}, bf16[128,1024]{1,0:T(8,128)(2,1)S(1)}, u32[]{:S(2)}, u32[]{:S(2)}) collective-permute-start(bf16[128,1024]{1,0:T(8,128)(2,1)S(1)} %get-tuple-element.96), channel_id=1, source_target_pairs={{0,16},{8,24},{16,0},{24,8},{1,17},{9,25},{17,1},{25,9},{2,18},{10... | collective-permute-start | bytes 786440 | tf_op jit(solution)/shard_map/ppermute | solution.py:65
  210.8 15.1 %collective-permute-start.66 = (bf16[128,1024]{1,0:T(8,128)(2,1)S(1)}, bf16[128,1024]{1,0:T(8,128)(2,1)S(1)}, u32[]{:S(2)}, u32[]{:S(2)}) collective-permute-start(bf16[128,1024]{1,0:T(8,128)(2,1)S(1)} %get-tuple-element.97), channel_id=1, source_target_pairs={{0,8},{8,0},{16,24},{24,16},{1,9},{9,1},{17,25},{25,17},{2,10},{10... | collective-permute-start | bytes 786440 | tf_op jit(solution)/shard_map/ppermute | solution.py:65
  214.7 15.1 %collective-permute-start.68 = (bf16[128,1024]{1,0:T(8,128)(2,1)S(1)}, bf16[128,1024]{1,0:T(8,128)(2,1)S(1)}, u32[]{:S(2)}, u32[]{:S(2)}) collective-permute-start(bf16[128,1024]{1,0:T(8,128)(2,1)S(1)} %get-tuple-element.98), channel_id=1, source_target_pairs={{0,24},{8,16},{16,8},{24,0},{1,25},{9,17},{17,9},{25,1},{2,26},{10... | collective-permute-start | bytes 786440 | tf_op jit(solution)/shard_map/ppermute | solution.py:65
  220.6 14.4 %collective-permute-start.67 = (bf16[128,1024]{1,0:T(8,128)(2,1)S(1)}, bf16[128,1024]{1,0:T(8,128)(2,1)S(1)}, u32[]{:S(2)}, u32[]{:S(2)}) collective-permute-start(bf16[128,1024]{1,0:T(8,128)(2,1)S(1)} %get-tuple-element.99), channel_id=1, source_target_pairs={{0,16},{8,24},{16,0},{24,8},{1,17},{9,25},{17,1},{25,9},{2,18},{10... | collective-permute-start | bytes 786440 | tf_op jit(solution)/shard_map/ppermute | solution.py:65
  222.9 18.4 %collective-permute-start.32 = (f32[1,1024,256]{2,1,0:T(8,128)S(1)}, f32[1,1024,256]{2,1,0:T(8,128)S(1)}, u32[]{:S(2)}, u32[]{:S(2)}) collective-permute-start(f32[1,1024,256]{2,1,0:T(8,128)S(1)} %slice.188), channel_id=1, source_target_pairs={{0,4},{4,0},{1,5},{5,1},{2,6},{6,2},{3,7},{7,3},{8,12},{12,8},{9,1... | collective-permute-start | bytes 3145736 | tf_op jit(solution)/shard_map/ppermute | solution.py:65
  225.9 26.8 %collective-permute-start.28 = (bf16[1024,256]{1,0:T(8,128)(2,1)}, bf16[1024,256]{1,0:T(8,128)(2,1)S(1)}, u32[]{:S(2)}, u32[]{:S(2)}) collective-permute-start(bf16[1024,256]{1,0:T(8,128)(2,1)} %get-tuple-element.82), channel_id=1, source_target_pairs={{3,2},{7,6},{11,10},{15,14},{19,18},{23,22},{27,26},{31,30}} | collective-permute-start | bytes 1572872 | tf_op jit(solution)/shard_map/ppermute | solution.py:55
  229.7 23.1 %collective-permute-start.26 = (bf16[1024,256]{1,0:T(8,128)(2,1)S(1)}, bf16[1024,256]{1,0:T(8,128)(2,1)}, u32[]{:S(2)}, u32[]{:S(2)}) collective-permute-start(bf16[1024,256]{1,0:T(8,128)(2,1)S(1)} %add_convert_fusion.11), channel_id=1, source_target_pairs={{0,1},{1,2},{4,5},{5,6},{8,9},{9,10},{12,13},{13,14},{16,17},{17,1... | collective-permute-start | bytes 1572872 | tf_op jit(solution)/shard_map/ppermute | solution.py:52
  234.9 39.5 %collective-permute-start.78 = (bf16[128,1024]{1,0:T(8,128)(2,1)}, bf16[128,1024]{1,0:T(8,128)(2,1)S(1)}, u32[]{:S(2)}, u32[]{:S(2)}) collective-permute-start(bf16[128,1024]{1,0:T(8,128)(2,1)} %get-tuple-element.55), channel_id=1, source_target_pairs={{0,16},{8,24},{16,0},{24,8},{1,17},{9,25},{17,1},{25,9},{2,18},{10... | collective-permute-start | bytes 786440 | tf_op jit(solution)/shard_map/ppermute | solution.py:65
  237.0 35.9 %collective-permute-start.77 = (bf16[128,1024]{1,0:T(8,128)(2,1)}, bf16[128,1024]{1,0:T(8,128)(2,1)S(1)}, u32[]{:S(2)}, u32[]{:S(2)}) collective-permute-start(bf16[128,1024]{1,0:T(8,128)(2,1)} %get-tuple-element.55), channel_id=1, source_target_pairs={{0,8},{8,0},{16,24},{24,16},{1,9},{9,1},{17,25},{25,17},{2,10},{10... | collective-permute-start | bytes 786440 | tf_op jit(solution)/shard_map/ppermute | solution.py:65
  241.3 33.3 %collective-permute-start.79 = (bf16[128,1024]{1,0:T(8,128)(2,1)}, bf16[128,1024]{1,0:T(8,128)(2,1)S(1)}, u32[]{:S(2)}, u32[]{:S(2)}) collective-permute-start(bf16[128,1024]{1,0:T(8,128)(2,1)} %get-tuple-element.55), channel_id=1, source_target_pairs={{0,24},{8,16},{16,8},{24,0},{1,25},{9,17},{17,9},{25,1},{2,26},{10... | collective-permute-start | bytes 786440 | tf_op jit(solution)/shard_map/ppermute | solution.py:65
  256.9 6.8 %collective-permute-start.40 = (f32[2,1024]{1,0:T(2,128)S(1)}, f32[2,1024]{1,0:T(2,128)S(1)}, u32[]{:S(2)}, u32[]{:S(2)}) collective-permute-start(f32[2,1024]{1,0:T(2,128)S(1)} %fusion.69), channel_id=1, source_target_pairs={{0,2},{1,3},{2,0},{3,1},{4,6},{5,7},{6,4},{7,5},{8,10},{9,11},{10,... | collective-permute-start | bytes 24584 | tf_op jit(solution)/shard_map/ppermute | solution.py:65
  262.7 21.8 %collective-permute-start.70 = (bf16[128,1024]{1,0:T(8,128)(2,1)S(1)}, bf16[128,1024]{1,0:T(8,128)(2,1)S(1)}, u32[]{:S(2)}, u32[]{:S(2)}) collective-permute-start(bf16[128,1024]{1,0:T(8,128)(2,1)S(1)} %copy-done.32), channel_id=1, source_target_pairs={{0,16},{8,24},{16,0},{24,8},{1,17},{9,25},{17,1},{25,9},{2,18},{10... | collective-permute-start | bytes 786440 | tf_op jit(solution)/shard_map/ppermute | solution.py:65
  271.5 9.2 %collective-permute-start.69 = (bf16[128,1024]{1,0:T(8,128)(2,1)S(1)}, bf16[128,1024]{1,0:T(8,128)(2,1)S(1)}, u32[]{:S(2)}, u32[]{:S(2)}) collective-permute-start(bf16[128,1024]{1,0:T(8,128)(2,1)S(1)} %copy-done.32), channel_id=1, source_target_pairs={{0,8},{8,0},{16,24},{24,16},{1,9},{9,1},{17,25},{25,17},{2,10},{10... | collective-permute-start | bytes 786440 | tf_op jit(solution)/shard_map/ppermute | solution.py:65
  272.9 32.5 %collective-permute-start.71 = (bf16[128,1024]{1,0:T(8,128)(2,1)S(1)}, bf16[128,1024]{1,0:T(8,128)(2,1)S(1)}, u32[]{:S(2)}, u32[]{:S(2)}) collective-permute-start(bf16[128,1024]{1,0:T(8,128)(2,1)S(1)} %copy-done.32), channel_id=1, source_target_pairs={{0,24},{8,16},{16,8},{24,0},{1,25},{9,17},{17,9},{25,1},{2,26},{10... | collective-permute-start | bytes 786440 | tf_op jit(solution)/shard_map/ppermute | solution.py:65
  274.5 13.5 %collective-permute-start.46 = (bf16[4,96,1024]{2,1,0:T(8,128)(2,1)S(1)}, bf16[4,96,1024]{2,1,0:T(8,128)(2,1)S(1)}, u32[]{:S(2)}, u32[]{:S(2)}) collective-permute-start(bf16[4,96,1024]{2,1,0:T(8,128)(2,1)S(1)} %fusion.35), channel_id=1, source_target_pairs={{0,4},{4,0},{1,5},{5,1},{2,6},{6,2},{3,7},{7,3},{8,12},{12,8},{9,1... | collective-permute-start | bytes 2359304 | tf_op jit(solution)/shard_map/ppermute | solution.py:65
  274.6 11.9 %collective-permute-start.29 = (bf16[1024,256]{1,0:T(8,128)(2,1)S(1)}, bf16[1024,256]{1,0:T(8,128)(2,1)S(1)}, u32[]{:S(2)}, u32[]{:S(2)}) collective-permute-start(bf16[1024,256]{1,0:T(8,128)(2,1)S(1)} %get-tuple-element.80), channel_id=1, source_target_pairs={{2,1},{3,2},{6,5},{7,6},{10,9},{11,10},{14,13},{15,14},{18,17},{19... | collective-permute-start | bytes 1572872 | tf_op jit(solution)/shard_map/ppermute | solution.py:55
  280.7 35.7 %collective-permute-start.27 = (bf16[1024,256]{1,0:T(8,128)(2,1)S(1)}, bf16[1024,256]{1,0:T(8,128)(2,1)S(1)}, u32[]{:S(2)}, u32[]{:S(2)}) collective-permute-start(bf16[1024,256]{1,0:T(8,128)(2,1)S(1)} %get-tuple-element.79), channel_id=1, source_target_pairs={{0,1},{1,2},{2,3},{4,5},{5,6},{6,7},{8,9},{9,10},{10,11},{12,13},{... | collective-permute-start | bytes 1572872 | tf_op jit(solution)/shard_map/ppermute | solution.py:52
  284.5 19.2 %collective-permute-start.33 = (bf16[1024,256]{1,0:T(8,128)(2,1)S(1)}, bf16[1024,256]{1,0:T(8,128)(2,1)S(1)}, u32[]{:S(2)}, u32[]{:S(2)}) collective-permute-start(bf16[1024,256]{1,0:T(8,128)(2,1)S(1)} %get-tuple-element.77), channel_id=1, source_target_pairs={{0,1},{4,5},{8,9},{12,13},{16,17},{20,21},{24,25},{28,29}} | collective-permute-start | bytes 1572872 | tf_op jit(solution)/shard_map/ppermute | solution.py:52
  286.7 30.3 %collective-permute-start.30 = (bf16[1024,256]{1,0:T(8,128)(2,1)S(1)}, bf16[1024,256]{1,0:T(8,128)(2,1)S(1)}, u32[]{:S(2)}, u32[]{:S(2)}) collective-permute-start(bf16[1024,256]{1,0:T(8,128)(2,1)S(1)} %add_convert_fusion.8), channel_id=1, source_target_pairs={{1,0},{2,1},{3,2},{5,4},{6,5},{7,6},{9,8},{10,9},{11,10},{13,12},{... | collective-permute-start | bytes 1572872 | tf_op jit(solution)/shard_map/ppermute | solution.py:55
  288.5 17.6 %collective-permute-start.47 = (bf16[96,1024]{1,0:T(8,128)(2,1)S(1)}, bf16[96,1024]{1,0:T(8,128)(2,1)S(1)}, u32[]{:S(2)}, u32[]{:S(2)}) collective-permute-start(bf16[96,1024]{1,0:T(8,128)(2,1)S(1)} %get-tuple-element.118), channel_id=1, source_target_pairs={{0,8},{8,0},{16,24},{24,16},{1,9},{9,1},{17,25},{25,17},{2,10},{10... | collective-permute-start | bytes 589832 | tf_op jit(solution)/shard_map/ppermute | solution.py:65
  303.7 6.8 %collective-permute-start.49 = (bf16[96,1024]{1,0:T(8,128)(2,1)S(1)}, bf16[96,1024]{1,0:T(8,128)(2,1)S(1)}, u32[]{:S(2)}, u32[]{:S(2)}) collective-permute-start(bf16[96,1024]{1,0:T(8,128)(2,1)S(1)} %get-tuple-element.119), channel_id=1, source_target_pairs={{0,24},{8,16},{16,8},{24,0},{1,25},{9,17},{17,9},{25,1},{2,26},{10... | collective-permute-start | bytes 589832 | tf_op jit(solution)/shard_map/ppermute | solution.py:65
  305.4 13.7 %collective-permute-start.36 = (bf16[1024,256]{1,0:T(8,128)(2,1)S(1)}, bf16[1024,256]{1,0:T(8,128)(2,1)S(1)}, u32[]{:S(2)}, u32[]{:S(2)}) collective-permute-start(bf16[1024,256]{1,0:T(8,128)(2,1)S(1)} %get-tuple-element.78), channel_id=1, source_target_pairs={{3,2},{7,6},{11,10},{15,14},{19,18},{23,22},{27,26},{31,30}} | collective-permute-start | bytes 1572872 | tf_op jit(solution)/shard_map/ppermute | solution.py:55
  306.1 14.2 %collective-permute-start.34 = (bf16[1024,256]{1,0:T(8,128)(2,1)S(1)}, bf16[1024,256]{1,0:T(8,128)(2,1)S(1)}, u32[]{:S(2)}, u32[]{:S(2)}) collective-permute-start(bf16[1024,256]{1,0:T(8,128)(2,1)S(1)} %add_convert_fusion.5), channel_id=1, source_target_pairs={{0,1},{1,2},{4,5},{5,6},{8,9},{9,10},{12,13},{13,14},{16,17},{17,1... | collective-permute-start | bytes 1572872 | tf_op jit(solution)/shard_map/ppermute | solution.py:52
  310.5 5.7 %collective-permute-start.48 = (bf16[96,1024]{1,0:T(8,128)(2,1)S(1)}, bf16[96,1024]{1,0:T(8,128)(2,1)S(1)}, u32[]{:S(2)}, u32[]{:S(2)}) collective-permute-start(bf16[96,1024]{1,0:T(8,128)(2,1)S(1)} %get-tuple-element.120), channel_id=1, source_target_pairs={{0,16},{8,24},{16,0},{24,8},{1,17},{9,25},{17,1},{25,9},{2,18},{10... | collective-permute-start | bytes 589832 | tf_op jit(solution)/shard_map/ppermute | solution.py:65
  316.2 15.9 %collective-permute-start.80 = (bf16[4,128,1024]{2,1,0:T(8,128)(2,1)S(1)}, bf16[4,128,1024]{2,1,0:T(8,128)(2,1)S(1)}, u32[]{:S(2)}, u32[]{:S(2)}) collective-permute-start(bf16[4,128,1024]{2,1,0:T(8,128)(2,1)S(1)} %bitcast_dynamic-update-slice_fusion), channel_id=1, source_target_pairs={{0,4},{4,0},{1,5},{5,1},{2,6},{6,2},{3,7},{7,3},{8,12},{12,8},{9,1... | collective-permute-start | bytes 3145736 | tf_op jit(solution)/shard_map/ppermute | solution.py:65
  316.4 16.2 %collective-permute-start.72 = (bf16[4,128,1024]{2,1,0:T(8,128)(2,1)S(1)}, bf16[4,128,1024]{2,1,0:T(8,128)(2,1)S(1)}, u32[]{:S(2)}, u32[]{:S(2)}) collective-permute-start(bf16[4,128,1024]{2,1,0:T(8,128)(2,1)S(1)} %bitcast_dynamic-update-slice_fusion.4), channel_id=1, source_target_pairs={{0,4},{4,0},{1,5},{5,1},{2,6},{6,2},{3,7},{7,3},{8,12},{12,8},{9,1... | collective-permute-start | bytes 3145736 | tf_op jit(solution)/shard_map/ppermute | solution.py:65
  317.0 14.3 %collective-permute-start.51 = (bf16[96,1024]{1,0:T(8,128)(2,1)S(1)}, bf16[96,1024]{1,0:T(8,128)(2,1)S(1)}, u32[]{:S(2)}, u32[]{:S(2)}) collective-permute-start(bf16[96,1024]{1,0:T(8,128)(2,1)S(1)} %get-tuple-element.67), channel_id=1, source_target_pairs={{0,16},{8,24},{16,0},{24,8},{1,17},{9,25},{17,1},{25,9},{2,18},{10... | collective-permute-start | bytes 589832 | tf_op jit(solution)/shard_map/ppermute | solution.py:65
  319.1 7.8 %collective-permute-start.50 = (bf16[96,1024]{1,0:T(8,128)(2,1)S(1)}, bf16[96,1024]{1,0:T(8,128)(2,1)S(1)}, u32[]{:S(2)}, u32[]{:S(2)}) collective-permute-start(bf16[96,1024]{1,0:T(8,128)(2,1)S(1)} %get-tuple-element.67), channel_id=1, source_target_pairs={{0,8},{8,0},{16,24},{24,16},{1,9},{9,1},{17,25},{25,17},{2,10},{10... | collective-permute-start | bytes 589832 | tf_op jit(solution)/shard_map/ppermute | solution.py:65
  320.3 11.7 %collective-permute-start.52 = (bf16[96,1024]{1,0:T(8,128)(2,1)S(1)}, bf16[96,1024]{1,0:T(8,128)(2,1)S(1)}, u32[]{:S(2)}, u32[]{:S(2)}) collective-permute-start(bf16[96,1024]{1,0:T(8,128)(2,1)S(1)} %get-tuple-element.67), channel_id=1, source_target_pairs={{0,24},{8,16},{16,8},{24,0},{1,25},{9,17},{17,9},{25,1},{2,26},{10... | collective-permute-start | bytes 589832 | tf_op jit(solution)/shard_map/ppermute | solution.py:65
  326.9 13.4 %collective-permute-start.35 = (bf16[1024,256]{1,0:T(8,128)(2,1)S(1)}, bf16[1024,256]{1,0:T(8,128)(2,1)S(1)}, u32[]{:S(2)}, u32[]{:S(2)}) collective-permute-start(bf16[1024,256]{1,0:T(8,128)(2,1)S(1)} %get-tuple-element.75), channel_id=1, source_target_pairs={{0,1},{1,2},{2,3},{4,5},{5,6},{6,7},{8,9},{9,10},{10,11},{12,13},{... | collective-permute-start | bytes 1572872 | tf_op jit(solution)/shard_map/ppermute | solution.py:52
  332.1 25.3 %collective-permute-start.53 = (bf16[4,96,1024]{2,1,0:T(8,128)(2,1)S(1)}, bf16[4,96,1024]{2,1,0:T(8,128)(2,1)S(1)}, u32[]{:S(2)}, u32[]{:S(2)}) collective-permute-start(bf16[4,96,1024]{2,1,0:T(8,128)(2,1)S(1)} %bitcast_dynamic-update-slice_fusion.8), channel_id=1, source_target_pairs={{0,4},{4,0},{1,5},{5,1},{2,6},{6,2},{3,7},{7,3},{8,12},{12,8},{9,1... | collective-permute-start | bytes 2359304 | tf_op jit(solution)/shard_map/ppermute | solution.py:65
  333.3 22.5 %collective-permute-start.38 = (bf16[1024,256]{1,0:T(8,128)(2,1)S(1)}, bf16[1024,256]{1,0:T(8,128)(2,1)S(1)}, u32[]{:S(2)}, u32[]{:S(2)}) collective-permute-start(bf16[1024,256]{1,0:T(8,128)(2,1)S(1)} %add_convert_fusion.2), channel_id=1, source_target_pairs={{1,0},{2,1},{3,2},{5,4},{6,5},{7,6},{9,8},{10,9},{11,10},{13,12},{... | collective-permute-start | bytes 1572872 | tf_op jit(solution)/shard_map/ppermute | solution.py:55
  362.2 6.6 %collective-permute-start.56 = (f32[2048]{0:T(1024)S(1)}, f32[2048]{0:T(1024)S(1)}, u32[]{:S(2)}, u32[]{:S(2)}) collective-permute-start(f32[2048]{0:T(1024)S(1)} %add.540), channel_id=1, source_target_pairs={{0,16},{8,24},{16,0},{24,8},{1,17},{9,25},{17,1},{25,9},{2,18},{10... | collective-permute-start | bytes 24584 | tf_op jit(solution)/shard_map/ppermute | solution.py:65
  (56 other events, 573.0 us)
